TPU v7x, 32 devices: a whole 2x2x4 slice. The times are simulated.
32 devices in a mesh: row: 8 (over y, x, core), col: 4 (over z).
Axes of the slice: x: 2, y: 2, z: 4, core: 2. Of those that a mesh axis runs over, the one named last changes fastest.
Arguments:
- features: bfloat16 [8192, 128], P(('row', 'col')), may hold values from -6 to 6
- weight: bfloat16 [128, 128], replicated, may hold values from -0.5 to 0.5
- bias: float32 [128], replicated, may hold values from -3 to 3
- node_scale: float32 [8192], P(('row', 'col')), may hold values from 0.04 to 0.2
- cotangent: bfloat16 [8192, 128], P(('row', 'col')), may hold values from -6 to 6
- tile_row: int32 [8, 4, 8], P('row', 'col'), may hold values from 0 to 3
- tile_col: int32 [8, 4, 8], P('row', 'col'), may hold values from 0 to 7
- tile_count: int32 [8, 4], P('row', 'col'), may hold values from 1 to 8, as said below
- tile_values: bfloat16 [8, 4, 8, 256, 256], P('row', 'col'), may hold values from 0 to 1
Outputs:
- activated: bfloat16 [8192, 128], P(('row', 'col'))
- feature_grad: bfloat16 [8192, 128], P(('row', 'col'))
- weight_grad: float32 [128, 128], replicated
- bias_grad: float32 [128], replicated
Inputs may be any that keep to these rules, and one draw needn't show every extreme that they name: `tile_count`: slots from this count on are ignored; in every draw some device has exactly 8 live slots.
All inputs are finite; a program needn't handle non-finite values.
Results may differ from a plain program's by a relative error of at most 0.015.
Values may be sent and summed in bfloat16 or wider, within the bound.
A program may use at most 64 MiB of HBM per device.

v0:
```python
import jax
import jax.numpy as jnp
from jax import lax
from jax.sharding import PartitionSpec as P

BLOCK = 256


def aggregate(blocks, rows_idx, cols_idx, weights, tiles, nbr, nbc):
    n_col = lax.axis_size("col")
    n_row = lax.axis_size("row")
    width = blocks.shape[1]
    x_rows = lax.all_gather(blocks, "col", axis=0, tiled=True).reshape(-1, BLOCK, width)
    x_cols = lax.all_gather(blocks, "row", axis=0, tiled=True).reshape(-1, BLOCK, width)
    row_terms = jnp.einsum(
        "tab,tbf->taf", tiles, x_cols[cols_idx], preferred_element_type=jnp.float32
    )
    col_terms = jnp.einsum(
        "tab,taf->tbf", tiles, x_rows[rows_idx], preferred_element_type=jnp.float32
    )
    row_part = jax.ops.segment_sum(row_terms * weights[:, None, None], rows_idx, num_segments=nbr)
    col_part = jax.ops.segment_sum(col_terms * weights[:, None, None], cols_idx, num_segments=nbc)
    row_in = lax.all_to_all(
        row_part.astype(jnp.bfloat16), "col", split_axis=0, concat_axis=0, tiled=True
    )
    total = jnp.sum(row_in.astype(jnp.float32), axis=0)
    col_in = lax.all_to_all(
        col_part.astype(jnp.bfloat16), "row", split_axis=0, concat_axis=0, tiled=True
    )
    total = total + jnp.sum(col_in.astype(jnp.float32), axis=0)
    return total


def shards(
    features, weight, bias, node_scale, cotangent, tile_row, tile_col, tile_count, tile_values
):
    n_col = lax.axis_size("col")
    n_row = lax.axis_size("row")
    row_pos = lax.axis_index("row")
    col_pos = lax.axis_index("col")
    per_dev = features.shape[0] // BLOCK
    nbr = n_col * per_dev
    nbc = n_row * per_dev
    rows_idx = tile_row[0, 0]
    cols_idx = tile_col[0, 0]
    count = tile_count[0, 0]
    tiles = tile_values[0, 0]
    slots = jnp.arange(rows_idx.shape[0], dtype=jnp.int32)
    glob_i = row_pos * nbr + rows_idx
    glob_j = (cols_idx // per_dev * n_col + col_pos) * per_dev + cols_idx % per_dev
    weights = jnp.where(slots < count, jnp.where(glob_i == glob_j, 0.5, 1.0), 0.0).astype(
        jnp.float32
    )
    scale = node_scale[:, None]
    projected = (scale * jnp.dot(features, weight, preferred_element_type=jnp.float32)).astype(
        jnp.bfloat16
    )
    summed = aggregate(projected, rows_idx, cols_idx, weights, tiles, nbr, nbc)
    preact = scale * (summed + projected.astype(jnp.float32)) + bias[None, :]
    activated = jax.nn.silu(preact).astype(jnp.bfloat16)
    sig = jax.nn.sigmoid(preact)
    delta = cotangent.astype(jnp.float32) * sig * (1.0 + preact * (1.0 - sig))
    scaled_delta = (scale * delta).astype(jnp.bfloat16)
    back = aggregate(scaled_delta, rows_idx, cols_idx, weights, tiles, nbr, nbc)
    proj_grad = (scale * (back + scaled_delta.astype(jnp.float32))).astype(jnp.bfloat16)
    feature_grad = jnp.dot(proj_grad, weight.T, preferred_element_type=jnp.float32).astype(
        jnp.bfloat16
    )
    local_weight = jnp.dot(features.T, proj_grad, preferred_element_type=jnp.float32)
    local_bias = jnp.sum(delta, axis=0)
    weight_grad, bias_grad = lax.psum((local_weight, local_bias), ("row", "col"))
    return (activated, feature_grad, weight_grad, bias_grad)


def solution(mesh):
    placed = (
        P(("row", "col"), None),
        P(),
        P(),
        P(("row", "col")),
        P(("row", "col"), None),
        P("row", "col", None),
        P("row", "col", None),
        P("row", "col"),
        P("row", "col", None, None, None),
    )
    return jax.shard_map(
        shards,
        mesh=mesh,
        in_specs=placed,
        out_specs=(P(("row", "col"), None), P(("row", "col"), None), P(), P()),
        check_vma=False,
    )
```

profile of v0, /device:TPU:0, one launch (start us, length us, event | category | flops | bytes accessed | tf_op | source)
XLA Modules:
  0.0 275.8 jit_solution(11787300515304883687)
XLA Ops:
  8.0 1.0 fusion.4
  9.0 11.3 %all_gather.12 = bf16[2048,128]{1,0:T(8,128)(2,1)S(1)} all-gather(bf16[256,128]{1,0:T(8,128)(2,1)S(1)} %fusion.4), channel_id=1, replica_groups=mesh['row'=8,'col'=4] {'row'}, dimensions={0}, use_global_device_ids=true | all-gather | bytes 589824 | tf_op jit(solution)/shard_map/all_gather | solution.py:14
  20.3 0.6 gather_fusion
  21.0 0.6 copy-done.7
  21.6 0.5 fusion.3
  22.1 0.3 copy.19
  22.5 1.3 scatter_fusion
  23.8 0.7 convert_element_type.49
  24.6 4.9 %all-to-all-start = ((bf16[4,256,128]{2,1,0:T(8,128)(2,1)}), bf16[4,256,128]{2,1,0:T(8,128)(2,1)}, u32[]{:S(2)}, u32[]{:S(2)}) async-start(bf16[4,256,128]{2,1,0:T(8,128)(2,1)} %convert_element_type.49), calls=%async_computation | async-start | bytes 524288 | tf_op jit(solution)/shard_map/all_to_all | solution.py:23
  29.5 18.0 %all_gather.13 = bf16[1024,128]{1,0:T(8,128)(2,1)S(1)} all-gather(bf16[256,128]{1,0:T(8,128)(2,1)S(1)} %fusion.4), channel_id=1, replica_groups=mesh['row'=8,'col'=4] {'col'}, dimensions={0}, use_global_device_ids=true | all-gather | bytes 327680 | tf_op jit(solution)/shard_map/all_gather | solution.py:13
  47.4 0.6 gather_fusion.1
  48.1 0.3 fusion.2
  48.4 0.3 copy.21
  48.8 0.1 broadcast.140.clone
  48.8 1.3 scatter_fusion.1
  50.2 0.9 convert_element_type.51
  51.0 3.5 %all-to-all-start.1 = ((bf16[8,256,128]{2,1,0:T(8,128)(2,1)}), bf16[8,256,128]{2,1,0:T(8,128)(2,1)S(1)}, u32[]{:S(2)}, u32[]{:S(2)}) async-start(bf16[8,256,128]{2,1,0:T(8,128)(2,1)} %convert_element_type.51), calls=%async_computation.1 | async-start | bytes 1048576 | tf_op jit(solution)/shard_map/all_to_all | solution.py:27
  54.5 1.0 convert_reduce_fusion.3
  55.6 8.6 %all-to-all-done.1 = bf16[8,256,128]{2,1,0:T(8,128)(2,1)S(1)} async-done(((bf16[8,256,128]{2,1,0:T(8,128)(2,1)}), bf16[8,256,128]{2,1,0:T(8,128)(2,1)S(1)}, u32[]{:S(2)}, u32[]{:S(2)}) %all-to-all-start.1) | async-done | bytes 524320 | tf_op jit(solution)/shard_map/all_to_all | solution.py:27
  64.2 0.1 convert_reduce_fusion.1
  64.3 1.3 fusion.12
  65.6 0.1 multiply_convert_fusion.1
  65.7 8.9 %all_gather.14 = bf16[2048,128]{1,0:T(8,128)(2,1)S(1)} all-gather(bf16[256,128]{1,0:T(8,128)(2,1)S(1)} %multiply_convert_fusion.1), channel_id=1, replica_groups=mesh['row'=8,'col'=4] {'row'}, dimensions={0}, use_global_device_ids=true | all-gather | bytes 589824 | tf_op jit(solution)/shard_map/all_gather | solution.py:14
  74.6 0.6 gather_fusion.2
  75.3 0.5 fusion.1
  75.8 0.3 copy.23
  76.1 1.3 scatter_fusion.2
  77.5 0.7 convert_element_type.57
  78.2 3.5 %all-to-all-start.2 = ((bf16[4,256,128]{2,1,0:T(8,128)(2,1)}), bf16[4,256,128]{2,1,0:T(8,128)(2,1)S(1)}, u32[]{:S(2)}, u32[]{:S(2)}) async-start(bf16[4,256,128]{2,1,0:T(8,128)(2,1)} %convert_element_type.57), calls=%async_computation.2 | async-start | bytes 524288 | tf_op jit(solution)/shard_map/all_to_all | solution.py:23
  81.8 18.0 %all_gather.15 = bf16[1024,128]{1,0:T(8,128)(2,1)S(1)} all-gather(bf16[256,128]{1,0:T(8,128)(2,1)S(1)} %copy-done.2), channel_id=1, replica_groups=mesh['row'=8,'col'=4] {'col'}, dimensions={0}, use_global_device_ids=true | all-gather | bytes 327680 | tf_op jit(solution)/shard_map/all_gather | solution.py:13
  99.7 0.6 gather_fusion.3
  100.4 0.3 fusion
  100.7 0.3 copy.25
  101.1 0.1 broadcast.140
  101.2 1.3 scatter_fusion.3
  102.5 0.9 convert_element_type.59
  103.4 3.5 %all-to-all-start.3 = ((bf16[8,256,128]{2,1,0:T(8,128)(2,1)}), bf16[8,256,128]{2,1,0:T(8,128)(2,1)S(1)}, u32[]{:S(2)}, u32[]{:S(2)}) async-start(bf16[8,256,128]{2,1,0:T(8,128)(2,1)} %convert_element_type.59), calls=%async_computation.3 | async-start | bytes 1048576 | tf_op jit(solution)/shard_map/all_to_all | solution.py:27
  106.9 0.0 all-reduce.2.cloned.1.call-start
  106.9 0.6 copy-done.10
  107.5 40.5 %psum.15 = f32[128]{0:T(128)} all-reduce(f32[128]{0:T(128)S(1)} %copy-done.10), channel_id=1, replica_groups=mesh['row'=8,'col'=4] {'row','col'}, use_global_device_ids=true, to_apply=%region_10.11 | all-reduce | flops 128 | bytes 1024 | tf_op jit(solution)/shard_map/psum | solution.py:71
  148.0 0.1 convert_reduce_fusion
  148.1 0.1 multiply_convert_fusion
  148.2 0.7 copy-done.3
  148.9 0.8 convolution_bitcast_fusion
  149.8 0.7 copy-done.4
  150.5 0.8 convolution_convert_fusion
  151.3 116.1 %all-reduce.2.cloned.1.call-done = f32[128,128]{0,1:T(8,128)} async-done(((f32[128,128]{0,1:T(8,128)}), f32[128,128]{0,1:T(8,128)}) %all-reduce.2.cloned.1.call-update) | async-done | bytes 65552 | tf_op jit(solution)/shard_map/psum | solution.py:71
  267.4 1.6 copy.26
  (30 shorter events, 0.2 us)
Async XLA Ops:
  7.2 14.5 %copy-start = (bf16[1,1,8,256,256]{4,3,2,1,0:T(8,128)(2,1)S(1)}, bf16[1,1,8,256,256]{4,3,2,1,0:T(8,128)(2,1)}, u32[]{:S(2)}) copy-start(bf16[1,1,8,256,256]{4,3,2,1,0:T(8,128)(2,1)} %param.17) | copy-start | bytes 3145732
  7.2 0.8 copy-start.6
  9.0 11.3 %copy-start.8 = (s32[1,1,8]{2,1,0:T(1,128)S(1)}, s32[1,1,8]{2,1,0:T(1,128)}, u32[]{:S(2)}) copy-start(s32[1,1,8]{2,1,0:T(1,128)} %param.15) | copy-start | bytes 100
  21.0 0.7 copy-start.7
  24.6 26.5 %all-to-all-start = ((bf16[4,256,128]{2,1,0:T(8,128)(2,1)}), bf16[4,256,128]{2,1,0:T(8,128)(2,1)}, u32[]{:S(2)}, u32[]{:S(2)}) async-start(bf16[4,256,128]{2,1,0:T(8,128)(2,1)} %convert_element_type.49), calls=%async_computation | async-start | bytes 524288 | tf_op jit(solution)/shard_map/all_to_all | solution.py:23
  51.0 13.2 %all-to-all-start.1 = ((bf16[8,256,128]{2,1,0:T(8,128)(2,1)}), bf16[8,256,128]{2,1,0:T(8,128)(2,1)S(1)}, u32[]{:S(2)}, u32[]{:S(2)}) async-start(bf16[8,256,128]{2,1,0:T(8,128)(2,1)} %convert_element_type.51), calls=%async_computation.1 | async-start | bytes 1048576 | tf_op jit(solution)/shard_map/all_to_all | solution.py:27
  55.6 8.7 %copy-start.5 = (bf16[256,128]{1,0:T(8,128)(2,1)S(1)}, bf16[256,128]{1,0:T(8,128)(2,1)}, u32[]{:S(2)}) copy-start(bf16[256,128]{1,0:T(8,128)(2,1)} %param.13) | copy-start | bytes 196612
  55.6 8.7 %copy-start.9 = (f32[128]{0:T(128)S(1)}, f32[128]{0:T(128)}, u32[]{:S(2)}) copy-start(f32[128]{0:T(128)} %param.11) | copy-start | bytes 1540
  65.7 8.9 %copy-start.1 = (bf16[256,128]{1,0:T(8,128)(2,1)}, bf16[256,128]{1,0:T(8,128)(2,1)S(1)}, u32[]{:S(2)}) copy-start(bf16[256,128]{1,0:T(8,128)(2,1)S(1)} %multiply_convert_fusion.1) | copy-start | bytes 196612
  78.2 3.5 %copy-start.2 = (bf16[256,128]{1,0:T(8,128)(2,1)S(1)}, bf16[256,128]{1,0:T(8,128)(2,1)}, u32[]{:S(2)}) copy-start(bf16[256,128]{1,0:T(8,128)(2,1)} %copy-done.1) | copy-start | bytes 196612
  78.2 25.2 %all-to-all-start.2 = ((bf16[4,256,128]{2,1,0:T(8,128)(2,1)}), bf16[4,256,128]{2,1,0:T(8,128)(2,1)S(1)}, u32[]{:S(2)}, u32[]{:S(2)}) async-start(bf16[4,256,128]{2,1,0:T(8,128)(2,1)} %convert_element_type.57), calls=%async_computation.2 | async-start | bytes 524288 | tf_op jit(solution)/shard_map/all_to_all | solution.py:23
  103.4 44.7 %all-to-all-start.3 = ((bf16[8,256,128]{2,1,0:T(8,128)(2,1)}), bf16[8,256,128]{2,1,0:T(8,128)(2,1)S(1)}, u32[]{:S(2)}, u32[]{:S(2)}) async-start(bf16[8,256,128]{2,1,0:T(8,128)(2,1)} %convert_element_type.59), calls=%async_computation.3 | async-start | bytes 1048576 | tf_op jit(solution)/shard_map/all_to_all | solution.py:27
  106.9 0.7 copy-start.10
  106.9 160.5 %all-reduce.2.cloned.1.call-start = ((), (), s32[]{:S(2)}) async-start(), calls=%async_computation.4 | async-start | bytes 131072 | tf_op jit(solution)/shard_map/psum | solution.py:71
  148.1 0.8 copy-start.3
  149.8 0.8 copy-start.4
Sparse Core Ops, SparseCore 0:
  149.9 117.4 all-reduce.1
where the time goes:
time: 278 us; the launch traced here: 276 us
  waiting for transfers between devices  125 us (45%)
  blocking collectives  96.6 us (35%)
  starting transfers between devices  15.4 us (6%)
  between operations  15.1 us (5%)
  other arithmetic  11.2 us (4%)
  local copies, waits for them, and re-layouts  8.43 us (3%)
  matrix products  4.28 us (2%)
    psum x1, waiting for transfers between devices, shards(): lax.psum((local_weight, local_bias), ('row', 'col'))  116 us
    psum x1, blocking collectives, shards(): lax.psum((local_weight, local_bias), ('row', 'col'))  40.5 us
    all_gather x2, blocking collectives, aggregate(): lax.all_gather(blocks, 'col', axis=0, tiled=True).reshape(-1, BLOCK, width)  35.9 us
    all_gather x2, blocking collectives, aggregate(): lax.all_gather(blocks, 'row', axis=0, tiled=True).reshape(-1, BLOCK, width)  20.2 us
    all_to_all x2, waiting for transfers between devices, aggregate(): lax.all_to_all(col_part.astype(jnp.bfloat16), 'row', split_axis=0, concat...  8.65 us
    all_to_all x2, starting transfers between devices, aggregate(): lax.all_to_all(row_part.astype(jnp.bfloat16), 'col', split_axis=0, concat...  8.42 us
    all_to_all x2, starting transfers between devices, aggregate(): lax.all_to_all(col_part.astype(jnp.bfloat16), 'row', split_axis=0, concat...  6.99 us
  transfers between devices with their start and end apart: 5, of which 2 were waited for; matrix products, arithmetic and copies ran while one was open for 3% of the time, Pallas kernels for 0%

commit v1 on v0

v1 whole, which is shorter than its diff:
```python
import functools

import jax
import jax.numpy as jnp
from jax import lax
from jax.experimental import pallas as pl
from jax.experimental.pallas import tpu as pltpu
from jax.sharding import PartitionSpec as P

BLOCK = 256
MESH = pl.DeviceIdType.MESH
F32 = jnp.float32
BF16 = jnp.bfloat16


def dot(a, b, dims=((1,), (0,))):
    return lax.dot_general(a, b, (dims, ((), ())), preferred_element_type=F32)


def layer_kernel(
    n_row, n_col, slots,
    rows_ref, cols_ref, count_ref, features_ref, weight_ref, bias_ref, scale_ref, cotangent_ref,
    tiles_hbm,
    act_ref, fgrad_ref, wgrad_ref, bgrad_ref,
    tiles, tiles_t, scale, terms, x_row0, x_row1, x_col0, x_col1, out_row, out_col, in_row, in_col,
    w_part, w_in, w_cross, w_all, load_sem, send_sem, recv_sem,
):
    r = lax.axis_index("row")
    c = lax.axis_index("col")
    width = features_ref.shape[1]
    chunk = width // n_row

    load = pltpu.make_async_copy(tiles_hbm, tiles, load_sem)
    load.start()

    row_peers = [lax.rem(r + k, n_row) for k in range(n_row)]
    col_peers = [lax.rem(c + k, n_col) for k in range(n_col)]

    barrier = pltpu.get_barrier_semaphore()
    for peer in row_peers[1:]:
        pl.semaphore_signal(barrier, inc=1, device_id=(peer, c), device_id_type=MESH)
    for peer in col_peers[1:]:
        pl.semaphore_signal(barrier, inc=1, device_id=(r, peer), device_id_type=MESH)

    def send_along_row(stage, k, src, dst):
        copy = pltpu.make_async_remote_copy(
            src_ref=src, dst_ref=dst.at[r],
            send_sem=send_sem.at[stage, k], recv_sem=recv_sem.at[stage, r],
            device_id=(row_peers[k], c), device_id_type=MESH)
        copy.start()
        sent.append(copy)

    def send_along_col(stage, k, src, dst):
        copy = pltpu.make_async_remote_copy(
            src_ref=src, dst_ref=dst.at[c],
            send_sem=send_sem.at[stage, n_row + k], recv_sem=recv_sem.at[stage, n_row + c],
            device_id=(r, col_peers[k]), device_id_type=MESH)
        copy.start()
        sent.append(copy)

    def wait_row(stage, dst, k):
        peer = row_peers[k]
        pltpu.make_async_remote_copy(
            src_ref=dst.at[peer], dst_ref=dst.at[peer],
            send_sem=send_sem.at[stage, k], recv_sem=recv_sem.at[stage, peer],
            device_id=(peer, c), device_id_type=MESH).wait_recv()

    def wait_col(stage, dst, k):
        peer = col_peers[k]
        pltpu.make_async_remote_copy(
            src_ref=dst.at[peer], dst_ref=dst.at[peer],
            send_sem=send_sem.at[stage, n_row + k], recv_sem=recv_sem.at[stage, n_row + peer],
            device_id=(r, peer), device_id_type=MESH).wait_recv()

    sent = []
    x_row = (x_row0, x_row1)
    x_col = (x_col0, x_col1)

    def gather(phase, block):
        xr, xc = x_row[phase], x_col[phase]
        xr[c] = block
        xc[r] = block
        if phase == 0:
            pl.semaphore_wait(barrier, n_row + n_col - 2)
        for k in range(1, max(n_row, n_col)):
            if k < n_row:
                send_along_row(phase, k, xc.at[r], xc)
            if k < n_col:
                send_along_col(phase, k, xr.at[c], xr)

    row_at = [rows_ref[t] for t in range(slots)]
    col_at = [cols_ref[t] for t in range(slots)]
    count = count_ref[0]
    weights = [
        jnp.where(
            t < count,
            jnp.where(r * n_col + row_at[t] == col_at[t] * n_col + c, 0.5, 1.0),
            0.0,
        ).astype(F32)
        for t in range(slots)
    ]

    def partial(at, index):
        total = None
        for t in range(slots):
            term = terms[t] * jnp.where(at[t] == index, weights[t], 0.0)
            total = term if total is None else total + term
        return total.astype(BF16)

    def spread(phase):
        xr, xc = x_row[phase], x_col[phase]
        for k in range(1, n_col):
            wait_col(phase, xr, k)
        for t in range(slots):
            terms[t] = dot(tiles_t[t], xr[row_at[t]])
        for k in range(1, n_row):
            out_col[phase, k] = partial(col_at, row_peers[k])
            send_along_row(2 + phase, k, out_col.at[phase, k], in_col.at[phase])
        in_col[phase, r] = partial(col_at, r)
        for k in range(1, n_row):
            wait_row(phase, xc, k)
        for t in range(slots):
            terms[t] = dot(tiles[t], xc[col_at[t]])
        for k in range(1, n_col):
            out_row[phase, k] = partial(row_at, col_peers[k])
            send_along_col(2 + phase, k, out_row.at[phase, k], in_row.at[phase])
        in_row[phase, c] = partial(row_at, c)

    def collect(phase, own):
        for k in range(1, n_row):
            wait_row(2 + phase, in_col.at[phase], k)
        for k in range(1, n_col):
            wait_col(2 + phase, in_row.at[phase], k)
        total = own
        for k in range(n_row):
            total = total + in_col[phase, k].astype(F32)
        for k in range(n_col):
            total = total + in_row[phase, k].astype(F32)
        return total

    scale[...] = jnp.broadcast_to(scale_ref[...], (width, BLOCK)).T
    scaled = (scale[...] * features_ref[...].astype(F32)).astype(BF16)
    gather(0, scaled)
    load.wait()
    for t in range(slots):
        tiles_t[t] = tiles[t].T
    spread(0)
    mixed = collect(0, scaled.astype(F32))
    high = mixed.astype(BF16)
    low = (mixed - high.astype(F32)).astype(BF16)
    product = dot(high, weight_ref[...]) + dot(low, weight_ref[...])
    preact = scale[...] * product + bias_ref[...]
    sig = 1.0 / (1.0 + jnp.exp(-preact))
    delta = cotangent_ref[...].astype(F32) * sig * (1.0 + preact * (1.0 - sig))
    scaled_delta = (scale[...] * delta).astype(BF16)
    gather(1, scaled_delta)
    act_ref[...] = (preact * sig).astype(BF16)

    local = dot(high, scaled_delta, ((0,), (0,)))
    local_bias = jnp.sum(delta, axis=0, keepdims=True)
    for k in range(n_row):
        w_part[k, :chunk, :] = local[k * chunk:(k + 1) * chunk]
        w_part[k, chunk:, :] = jnp.broadcast_to(local_bias, (8, width))
    for k in range(1, n_row):
        send_along_row(4, k, w_part.at[row_peers[k]], w_in)
    w_in[r] = w_part[r]
    for k in range(1, n_row):
        wait_row(4, w_in, k)
    summed = w_in[0]
    for k in range(1, n_row):
        summed = summed + w_in[k]
    w_cross[c] = summed
    for k in range(1, n_col):
        send_along_col(4, k, w_cross.at[c], w_cross)
    spread(1)
    for k in range(1, n_col):
        wait_col(4, w_cross, k)
    summed = w_cross[0]
    for k in range(1, n_col):
        summed = summed + w_cross[k]
    w_all[r] = summed
    for k in range(1, n_row):
        send_along_row(5, k, w_all.at[r], w_all)
    bgrad_ref[...] = summed[chunk:chunk + 1]

    back = collect(1, scaled_delta.astype(F32))
    proj_grad = (scale[...] * back).astype(BF16)
    fgrad_ref[...] = dot(proj_grad, weight_ref[...], ((1,), (1,))).astype(BF16)
    for k in range(1, n_row):
        wait_row(5, w_all, k)
    for k in range(n_row):
        wgrad_ref[k * chunk:(k + 1) * chunk, :] = w_all[k, :chunk, :]
    for copy in sent:
        copy.wait_send()


def shards(
    n_row, n_col,
    features, weight, bias, node_scale, cotangent, tile_row, tile_col, tile_count, tile_values
):
    width = features.shape[1]
    slots = tile_row.shape[-1]
    assert features.shape[0] == BLOCK
    chunk = width // n_row
    vmem = pl.BlockSpec(memory_space=pltpu.VMEM)
    smem = pl.BlockSpec(memory_space=pltpu.SMEM)
    peers = n_row + n_col
    act, fgrad, wgrad, bgrad = pl.pallas_call(
        functools.partial(layer_kernel, n_row, n_col, slots),
        out_shape=(
            jax.ShapeDtypeStruct((BLOCK, width), BF16),
            jax.ShapeDtypeStruct((BLOCK, width), BF16),
            jax.ShapeDtypeStruct((width, width), F32),
            jax.ShapeDtypeStruct((1, width), F32),
        ),
        in_specs=[smem, smem, smem, vmem, vmem, vmem, vmem, vmem, pl.BlockSpec(memory_space=pl.ANY)],
        out_specs=(vmem, vmem, vmem, vmem),
        scratch_shapes=[
            pltpu.VMEM((slots, BLOCK, BLOCK), BF16),
            pltpu.VMEM((slots, BLOCK, BLOCK), BF16),
            pltpu.VMEM((BLOCK, width), F32),
            pltpu.VMEM((slots, BLOCK, width), F32),
            pltpu.VMEM((n_col, BLOCK, width), BF16),
            pltpu.VMEM((n_col, BLOCK, width), BF16),
            pltpu.VMEM((n_row, BLOCK, width), BF16),
            pltpu.VMEM((n_row, BLOCK, width), BF16),
            pltpu.VMEM((2, n_col, BLOCK, width), BF16),
            pltpu.VMEM((2, n_row, BLOCK, width), BF16),
            pltpu.VMEM((2, n_col, BLOCK, width), BF16),
            pltpu.VMEM((2, n_row, BLOCK, width), BF16),
            pltpu.VMEM((n_row, chunk + 8, width), F32),
            pltpu.VMEM((n_row, chunk + 8, width), F32),
            pltpu.VMEM((n_col, chunk + 8, width), F32),
            pltpu.VMEM((n_row, chunk + 8, width), F32),
            pltpu.SemaphoreType.DMA,
            pltpu.SemaphoreType.DMA((6, peers)),
            pltpu.SemaphoreType.DMA((6, peers)),
        ],
        compiler_params=pltpu.CompilerParams(
            collective_id=0, has_side_effects=True, vmem_limit_bytes=48 * 1024 * 1024
        ),
    )(
        tile_row.reshape(slots), tile_col.reshape(slots), tile_count.reshape(1),
        features, weight, bias.reshape(1, width), node_scale.reshape(1, BLOCK), cotangent,
        tile_values.reshape(slots, BLOCK, BLOCK),
    )
    return act, fgrad, wgrad, bgrad.reshape(width)


def solution(mesh):
    placed = (
        P(("row", "col"), None),
        P(),
        P(),
        P(("row", "col")),
        P(("row", "col"), None),
        P("row", "col", None),
        P("row", "col", None),
        P("row", "col"),
        P("row", "col", None, None, None),
    )
    return jax.shard_map(
        functools.partial(shards, mesh.shape["row"], mesh.shape["col"]),
        mesh=mesh,
        in_specs=placed,
        out_specs=(P(("row", "col"), None), P(("row", "col"), None), P(), P()),
        check_vma=False,
    )
```

time: 278 us -> 48.3 us (0.17)
  waiting for transfers between devices: 125 us -> 0 us
  blocking collectives: 96.6 us -> 0 us
  Pallas kernels: 0 us -> 39.9 us
  starting transfers between devices: 15.4 us -> 0 us
  between operations: 15.1 us -> 1.33 us
  other arithmetic: 11.2 us -> 0 us
  matrix products: 4.28 us -> 0 us
    psum x1 -> x0, waiting for transfers between devices: 116 us -> none  [shards(): lax.psum((local_weight, local_bias), ('row', 'col'))]
    all_gather x4 -> x0, blocking collectives: 56.1 us -> none  [the longest x2 35.9 us: aggregate(): lax.all_gather(blocks, 'col', axis=0, tiled=True).reshape(-1, BLOCK, width)]
    psum x1 -> x0, blocking collectives: 40.5 us -> none  [shards(): lax.psum((local_weight, local_bias), ('row', 'col'))]
    pallas_call x0 -> x1, Pallas kernels: none -> 39.9 us  [shards(): pl.pallas_call(functools.partial(layer_kernel, n_row, n_col, slots), out_...]
    all_to_all x4 -> x0, starting transfers between devices: 15.4 us -> none  [the longest x2 8.42 us: aggregate(): lax.all_to_all(row_part.astype(jnp.bfloat16), 'col', split_axis=0, concat...]
    all_to_all x4 -> x0, waiting for transfers between devices: 8.66 us -> none  [the longest x2 8.65 us: aggregate(): lax.all_to_all(col_part.astype(jnp.bfloat16), 'row', split_axis=0, concat...]
    scatter-add x4 -> x0, other arithmetic: 5.29 us -> none  [the longest x2 2.65 us: aggregate(): jax.ops.segment_sum(col_terms * weights[:, None, None], cols_idx, num_seg...]
    dot_general x7 -> x0, matrix products: 4.28 us -> none  [the longest x1 1 us: shards(): jnp.dot(features, weight, preferred_element_type=jnp.float32)]
  transfers between devices with their start and end apart: 5 -> 0, of which waited for: 2 -> 0; matrix products, arithmetic and copies ran while one was open for 3% -> 0% of each run, Pallas kernels for 0% -> 0%
where the time goes in v1:
time: 48.3 us; the launch traced here: 48 us
  Pallas kernels  39.9 us (83%)
  local copies, waits for them, and re-layouts  6.74 us (14%)
  between operations  1.33 us (3%)
    pallas_call x1, Pallas kernels, shards(): pl.pallas_call(functools.partial(layer_kernel, n_row, n_col, slots), out_...  39.9 us
    unnamed x20, local copies, waits for them, and re-layouts  6.74 us

profile of v1, /device:TPU:0, one launch (start us, length us, event | category | flops | bytes accessed | tf_op | source)
XLA Modules:
  0.0 48.0 jit_solution(17144295321194720714)
XLA Ops:
  1.3 0.0 copy-start.6
  1.3 0.0 copy-start.7
  1.3 0.0 copy-start.4
  1.3 0.0 copy-start.5
  1.3 0.6 %copy-done.6 = s32[1,1,8]{2,1,0:T(1,128)S(1)} copy-done((s32[1,1,8]{2,1,0:T(1,128)S(1)}, s32[1,1,8]{2,1,0:T(1,128)}, u32[]{:S(2)}) %copy-start.6) | copy-done | bytes 56
  1.9 0.0 copy-done.7
  2.0 0.0 copy-done.4
  2.0 0.0 copy-done.5
  2.0 0.0 copy-start
  2.0 1.2 %copy-done = bf16[1,1,8,256,256]{4,3,2,1,0:T(8,128)(2,1)S(1)} copy-done((bf16[1,1,8,256,256]{4,3,2,1,0:T(8,128)(2,1)S(1)}, bf16[1,1,8,256,256]{4,3,2,1,0:T(8,128)(2,1)}, u32[]{:S(2)}) %copy-start) | copy-done | bytes 1048600
  3.2 0.0 copy-start.1
  3.2 0.8 %copy-done.1 = bf16[256,128]{1,0:T(8,128)(2,1)S(1)} copy-done((bf16[256,128]{1,0:T(8,128)(2,1)S(1)}, bf16[256,128]{1,0:T(8,128)(2,1)}, u32[]{:S(2)}) %copy-start.1) | copy-done | bytes 65560
  4.1 0.0 copy-start.2
  4.1 0.8 %copy-done.2 = bf16[256,128]{1,0:T(8,128)(2,1)S(1)} copy-done((bf16[256,128]{1,0:T(8,128)(2,1)S(1)}, bf16[256,128]{1,0:T(8,128)(2,1)}, u32[]{:S(2)}) %copy-start.2) | copy-done | bytes 65560
  4.9 0.0 copy-start.3
  4.9 0.8 %copy-done.3 = bf16[128,128]{1,0:T(8,128)(2,1)S(1)} copy-done((bf16[128,128]{1,0:T(8,128)(2,1)S(1)}, bf16[128,128]{1,0:T(8,128)(2,1)}, u32[]{:S(2)}) %copy-start.3) | copy-done | bytes 32792
  5.7 39.9 %shard_map.120 = (bf16[256,128]{1,0:T(8,128)(2,1)S(1)}, bf16[256,128]{1,0:T(8,128)(2,1)S(1)}, f32[128,128]{1,0:T(8,128)S(1)}, f32[1,128]{1,0:T(1,128)S(1)}) custom-call(s32[8]{0:T(128)S(1)} %bitcast.10, s32[8]{0:T(128)S(1)} %bitcast.11, s32[1]{0:T(128)} %bitcast.7.count_ref, bf16[256,128]{1,0:T(8,128)(2,1)S(1)} %copy-done.1, bf16[128,128]{1,0:T(8,128)(2,1)S(1)} %copy-done.3, ...), custom_call_target="tpu_custom_call" | custom-call | tf_op jit(solution)/shard_map/pallas_call | solution.py:208
  45.6 0.6 %copy.18 = bf16[256,128]{1,0:T(8,128)(2,1)} copy(bf16[256,128]{1,0:T(8,128)(2,1)S(1)} %get-tuple-element.16) | data formatting | bytes 131072
  46.2 0.6 %copy.19 = bf16[256,128]{1,0:T(8,128)(2,1)} copy(bf16[256,128]{1,0:T(8,128)(2,1)S(1)} %get-tuple-element.17) | data formatting | bytes 131072
  46.8 0.6 %copy.20 = f32[128,128]{1,0:T(8,128)} copy(f32[128,128]{1,0:T(8,128)S(1)} %get-tuple-element.18) | data formatting | bytes 131072
  47.5 0.5 %copy.21 = f32[128]{0:T(128)} copy(f32[128]{0:T(128)S(1)} %bitcast.13) | data formatting | bytes 1024
Async XLA Ops:
  1.3 0.7 %copy-start.6 = (s32[1,1,8]{2,1,0:T(1,128)S(1)}, s32[1,1,8]{2,1,0:T(1,128)}, u32[]{:S(2)}) copy-start(s32[1,1,8]{2,1,0:T(1,128)} %param.15) | copy-start | bytes 100
  1.3 0.7 %copy-start.7 = (f32[128]{0:T(128)S(1)}, f32[128]{0:T(128)}, u32[]{:S(2)}) copy-start(f32[128]{0:T(128)} %param.11) | copy-start | bytes 1540
  1.3 0.7 %copy-start.4 = (f32[256]{0:T(256)S(1)}, f32[256]{0:T(256)}, u32[]{:S(2)}) copy-start(f32[256]{0:T(256)} %param.12) | copy-start | bytes 3076
  1.3 0.7 %copy-start.5 = (s32[1,1,8]{2,1,0:T(1,128)S(1)}, s32[1,1,8]{2,1,0:T(1,128)}, u32[]{:S(2)}) copy-start(s32[1,1,8]{2,1,0:T(1,128)} %param.14) | copy-start | bytes 100
  2.0 1.2 %copy-start = (bf16[1,1,8,256,256]{4,3,2,1,0:T(8,128)(2,1)S(1)}, bf16[1,1,8,256,256]{4,3,2,1,0:T(8,128)(2,1)}, u32[]{:S(2)}) copy-start(bf16[1,1,8,256,256]{4,3,2,1,0:T(8,128)(2,1)} %param.17) | copy-start | bytes 3145732
  3.2 0.8 %copy-start.1 = (bf16[256,128]{1,0:T(8,128)(2,1)S(1)}, bf16[256,128]{1,0:T(8,128)(2,1)}, u32[]{:S(2)}) copy-start(bf16[256,128]{1,0:T(8,128)(2,1)} %features_ref.1) | copy-start | bytes 196612
  4.1 0.8 %copy-start.2 = (bf16[256,128]{1,0:T(8,128)(2,1)S(1)}, bf16[256,128]{1,0:T(8,128)(2,1)}, u32[]{:S(2)}) copy-start(bf16[256,128]{1,0:T(8,128)(2,1)} %cotangent_ref.1) | copy-start | bytes 196612
  4.9 0.8 %copy-start.3 = (bf16[128,128]{1,0:T(8,128)(2,1)S(1)}, bf16[128,128]{1,0:T(8,128)(2,1)}, u32[]{:S(2)}) copy-start(bf16[128,128]{1,0:T(8,128)(2,1)} %weight_ref.1) | copy-start | bytes 98308

commit v2 on v1

v2 whole, which is shorter than its diff:
```python
import functools

import jax
import jax.numpy as jnp
from jax import lax
from jax.experimental import pallas as pl
from jax.experimental.pallas import tpu as pltpu
from jax.sharding import PartitionSpec as P

BLOCK = 256
VMEM_LIMIT = 60 * 1024 * 1024
MESH = pl.DeviceIdType.MESH
F32 = jnp.float32
BF16 = jnp.bfloat16


def dot(a, b, dims=((1,), (0,))):
    return lax.dot_general(a, b, (dims, ((), ())), preferred_element_type=F32)


def layer_kernel(
    n_row, n_col, slots, halves,
    rows_hbm, cols_hbm, count_hbm, features_hbm, weight_hbm, bias_hbm, scale_hbm, cotangent_hbm,
    tiles_hbm,
    act_hbm, fgrad_hbm, wgrad_hbm, bgrad_hbm,
    act_ref, fgrad_ref, wgrad_ref, bgrad_ref, store_sem, rows_ref, cols_ref, count_ref, features, weight, bias, scale_ref, cotangent,
    tiles, tiles_t, terms, out_row, out_col, in_row, in_col,
    w_part, w_in, w_cross, w_all, load_sem, send_sem, recv_sem, *blocks,
):
    r = lax.axis_index("row")
    c = lax.axis_index("col")
    width = features.shape[1]
    chunk = width // n_row
    part = width // halves

    pairs = (
        (features_hbm, features), (scale_hbm, scale_ref), (rows_hbm, rows_ref), (cols_hbm, cols_ref),
        (count_hbm, count_ref), (tiles_hbm, tiles), (weight_hbm, weight), (bias_hbm, bias),
        (cotangent_hbm, cotangent),
    )
    loads = [pltpu.make_async_copy(src, dst, load_sem.at[n]) for n, (src, dst) in enumerate(pairs)]
    for load in loads:
        load.start()

    row_peers = [lax.rem(r + k, n_row) for k in range(n_row)]
    col_peers = [lax.rem(c + k, n_col) for k in range(n_col)]

    barrier = pltpu.get_barrier_semaphore()
    for peer in row_peers[1:]:
        pl.semaphore_signal(barrier, inc=1, device_id=(peer, c), device_id_type=MESH)
    for peer in col_peers[1:]:
        pl.semaphore_signal(barrier, inc=1, device_id=(r, peer), device_id_type=MESH)

    sent = []

    def store(n, src, dst):
        copy = pltpu.make_async_copy(src, dst, store_sem.at[n])
        copy.start()
        stores.append(copy)

    stores = []

    def send_along_row(stage, k, src, dst):
        copy = pltpu.make_async_remote_copy(
            src_ref=src, dst_ref=dst.at[r],
            send_sem=send_sem.at[stage, k], recv_sem=recv_sem.at[stage, r],
            device_id=(row_peers[k], c), device_id_type=MESH)
        copy.start()
        sent.append(copy)

    def send_along_col(stage, k, src, dst):
        copy = pltpu.make_async_remote_copy(
            src_ref=src, dst_ref=dst.at[c],
            send_sem=send_sem.at[stage, n_row + k], recv_sem=recv_sem.at[stage, n_row + c],
            device_id=(r, col_peers[k]), device_id_type=MESH)
        copy.start()
        sent.append(copy)

    def wait_row(stage, dst, k):
        peer = row_peers[k]
        pltpu.make_async_remote_copy(
            src_ref=dst.at[peer], dst_ref=dst.at[peer],
            send_sem=send_sem.at[stage, k], recv_sem=recv_sem.at[stage, peer],
            device_id=(peer, c), device_id_type=MESH).wait_recv()

    def wait_col(stage, dst, k):
        peer = col_peers[k]
        pltpu.make_async_remote_copy(
            src_ref=dst.at[peer], dst_ref=dst.at[peer],
            send_sem=send_sem.at[stage, n_row + k], recv_sem=recv_sem.at[stage, n_row + peer],
            device_id=(r, peer), device_id_type=MESH).wait_recv()

    x_row = blocks[: 2 * halves]
    x_col = blocks[2 * halves:]
    spread_at = 2 * halves
    sum_at = 4 * halves

    def gather(step, block):
        xr, xc = x_row[step], x_col[step]
        xr[c] = block
        xc[r] = block
        if step == 0:
            pl.semaphore_wait(barrier, n_row + n_col - 2)
        for k in range(1, max(n_row, n_col)):
            if k < n_col:
                send_along_col(step, k, xr.at[c], xr)
            if k < n_row:
                send_along_row(step, k, xc.at[r], xc)

    def partial(at, index, weights):
        total = None
        for t in range(slots):
            term = terms[t] * jnp.where(at[t] == index, weights[t], 0.0)
            total = term if total is None else total + term
        return total.astype(BF16)

    def spread(step, row_at, col_at, weights):
        xr, xc = x_row[step], x_col[step]
        for k in range(1, n_col):
            wait_col(step, xr, k)
        for t in range(slots):
            terms[t] = dot(xr[row_at[t]], tiles[t])
        for k in range(1, n_row):
            out_col[step, k] = partial(col_at, row_peers[k], weights)
            send_along_row(spread_at + step, k, out_col.at[step, k], in_col.at[step])
        in_col[step, r] = partial(col_at, r, weights)
        for k in range(1, n_row):
            wait_row(step, xc, k)
        for t in range(slots):
            terms[t] = dot(xc[col_at[t]], tiles_t[t])
        for k in range(1, n_col):
            out_row[step, k] = partial(row_at, col_peers[k], weights)
            send_along_col(spread_at + step, k, out_row.at[step, k], in_row.at[step])
        in_row[step, c] = partial(row_at, c, weights)

    def collect(step, own):
        for k in range(1, n_row):
            wait_row(spread_at + step, in_col.at[step], k)
        for k in range(1, n_col):
            wait_col(spread_at + step, in_row.at[step], k)
        total = own.astype(F32)
        for k in range(n_row):
            total = total + in_col[step, k].astype(F32)
        for k in range(n_col):
            total = total + in_row[step, k].astype(F32)
        return total

    for load in loads[:2]:
        load.wait()
    scale = scale_ref[...]
    scaled = (scale * features[...].astype(F32).T).astype(BF16)
    for h in range(halves):
        gather(h, scaled[h * part:(h + 1) * part])
    for load in loads[2:]:
        load.wait()
    row_at = [rows_ref[t] for t in range(slots)]
    col_at = [cols_ref[t] for t in range(slots)]
    count = count_ref[0]
    weights = [
        jnp.where(
            t < count,
            jnp.where(r * n_col + row_at[t] == col_at[t] * n_col + c, 0.5, 1.0),
            0.0,
        ).astype(F32)
        for t in range(slots)
    ]
    for t in range(slots):
        tiles_t[t] = tiles[t].T
    for h in range(halves):
        spread(h, row_at, col_at, weights)
    mixed = jnp.concatenate(
        [collect(h, scaled[h * part:(h + 1) * part]) for h in range(halves)], axis=0)
    high = mixed.astype(BF16)
    low = (mixed - high.astype(F32)).astype(BF16)
    weight_t = weight[...].T
    bias_t = jnp.broadcast_to(bias[...], (BLOCK, width)).T
    cotangent_t = cotangent[...].astype(F32).T
    acts, deltas, scaled_deltas = [], [], []
    for h in range(halves):
        rows = slice(h * part, (h + 1) * part)
        product = dot(weight_t[rows], high) + dot(weight_t[rows], low)
        preact = scale * product + bias_t[rows]
        sig = 1.0 / (1.0 + jnp.exp(-preact))
        delta = cotangent_t[rows] * sig * (1.0 + preact * (1.0 - sig))
        scaled_delta = (scale * delta).astype(BF16)
        gather(halves + h, scaled_delta)
        acts.append(preact * sig)
        deltas.append(delta)
        scaled_deltas.append(scaled_delta)

    local = dot(high, jnp.concatenate(scaled_deltas, axis=0), ((1,), (1,)))
    local_bias = jnp.sum(jnp.concatenate(deltas, axis=0).T, axis=0, keepdims=True)
    for k in range(n_row):
        w_part[k, :chunk, :] = local[k * chunk:(k + 1) * chunk]
        w_part[k, chunk:, :] = jnp.broadcast_to(local_bias, (8, width))
    for k in range(1, n_row):
        send_along_row(sum_at, k, w_part.at[row_peers[k]], w_in)
    w_in[r] = w_part[r]
    act_ref[...] = jnp.concatenate(acts, axis=0).T.astype(BF16)
    store(0, act_ref, act_hbm)
    for h in range(halves - 1):
        spread(halves + h, row_at, col_at, weights)
    for k in range(1, n_row):
        wait_row(sum_at, w_in, k)
    summed = w_in[0]
    for k in range(1, n_row):
        summed = summed + w_in[k]
    w_cross[c] = summed
    for k in range(1, n_col):
        send_along_col(sum_at, k, w_cross.at[c], w_cross)
    spread(2 * halves - 1, row_at, col_at, weights)
    for k in range(1, n_col):
        wait_col(sum_at, w_cross, k)
    summed = w_cross[0]
    for k in range(1, n_col):
        summed = summed + w_cross[k]
    w_all[r] = summed
    for k in range(1, n_row):
        send_along_row(sum_at + 1, k, w_all.at[r], w_all)
    bgrad_ref[...] = summed[chunk:chunk + 1]
    store(3, bgrad_ref, bgrad_hbm)

    fgrad_t = None
    for h in range(halves):
        proj_grad = (scale * collect(halves + h, scaled_deltas[h])).astype(BF16)
        term = dot(weight[:, h * part:(h + 1) * part], proj_grad)
        fgrad_t = term if fgrad_t is None else fgrad_t + term
    fgrad_ref[...] = fgrad_t.T.astype(BF16)
    store(1, fgrad_ref, fgrad_hbm)
    for k in range(1, n_row):
        wait_row(sum_at + 1, w_all, k)
    for k in range(n_row):
        wgrad_ref[k * chunk:(k + 1) * chunk, :] = w_all[k, :chunk, :]
    store(2, wgrad_ref, wgrad_hbm)
    for copy in sent:
        copy.wait_send()
    for copy in stores:
        copy.wait()


def finish_kernel(count, *refs):
    sem = refs[-1]
    copies = [
        pltpu.make_async_copy(refs[n], refs[count + n], sem.at[n]) for n in range(count)
    ]
    for copy in copies:
        copy.start()
    for copy in copies:
        copy.wait()


def shards(
    n_row, n_col,
    features, weight, bias, node_scale, cotangent, tile_row, tile_col, tile_count, tile_values
):
    width = features.shape[1]
    slots = tile_row.shape[-1]
    assert features.shape[0] == BLOCK
    chunk = width // n_row
    halves = 2
    part = width // halves
    hbm = pl.BlockSpec(memory_space=pltpu.HBM)
    peers = n_row + n_col
    shapes = (
        jax.ShapeDtypeStruct((BLOCK, width), BF16),
        jax.ShapeDtypeStruct((BLOCK, width), BF16),
        jax.ShapeDtypeStruct((width, width), F32),
        jax.ShapeDtypeStruct((1, width), F32),
    )
    results = pl.pallas_call(
        functools.partial(layer_kernel, n_row, n_col, slots, halves),
        out_shape=shapes,
        in_specs=[hbm] * 9,
        out_specs=(hbm,) * 4,
        scratch_shapes=[pltpu.VMEM(shape.shape, shape.dtype) for shape in shapes]
        + [
            pltpu.SemaphoreType.DMA((4,)),
            pltpu.SMEM((slots,), jnp.int32),
            pltpu.SMEM((slots,), jnp.int32),
            pltpu.SMEM((1,), jnp.int32),
            pltpu.VMEM((BLOCK, width), BF16),
            pltpu.VMEM((width, width), BF16),
            pltpu.VMEM((1, width), F32),
            pltpu.VMEM((1, BLOCK), F32),
            pltpu.VMEM((BLOCK, width), BF16),
            pltpu.VMEM((slots, BLOCK, BLOCK), BF16),
            pltpu.VMEM((slots, BLOCK, BLOCK), BF16),
            pltpu.VMEM((slots, part, BLOCK), F32),
            pltpu.VMEM((2 * halves, n_col, part, BLOCK), BF16),
            pltpu.VMEM((2 * halves, n_row, part, BLOCK), BF16),
            pltpu.VMEM((2 * halves, n_col, part, BLOCK), BF16),
            pltpu.VMEM((2 * halves, n_row, part, BLOCK), BF16),
            pltpu.VMEM((n_row, chunk + 8, width), F32),
            pltpu.VMEM((n_row, chunk + 8, width), F32),
            pltpu.VMEM((n_col, chunk + 8, width), F32),
            pltpu.VMEM((n_row, chunk + 8, width), F32),
            pltpu.SemaphoreType.DMA((9,)),
            pltpu.SemaphoreType.DMA((4 * halves + 2, peers)),
            pltpu.SemaphoreType.DMA((4 * halves + 2, peers)),
        ]
        + [pltpu.VMEM((n_col, part, BLOCK), BF16)] * (2 * halves)
        + [pltpu.VMEM((n_row, part, BLOCK), BF16)] * (2 * halves),
        compiler_params=pltpu.CompilerParams(
            collective_id=0, has_side_effects=True, vmem_limit_bytes=VMEM_LIMIT
        ),
    )(
        tile_row.reshape(slots), tile_col.reshape(slots), tile_count.reshape(1),
        features, weight, bias.reshape(1, width), node_scale.reshape(1, BLOCK), cotangent,
        tile_values.reshape(slots, BLOCK, BLOCK),
    )
    act, fgrad, wgrad, bgrad = pl.pallas_call(
        functools.partial(finish_kernel, 4),
        out_shape=shapes,
        in_specs=[pl.BlockSpec(memory_space=pl.ANY)] * 4,
        out_specs=(hbm,) * 4,
        scratch_shapes=[pltpu.SemaphoreType.DMA((4,))],
        compiler_params=pltpu.CompilerParams(vmem_limit_bytes=VMEM_LIMIT),
    )(*results)
    return act, fgrad, wgrad, bgrad.reshape(width)


def solution(mesh):
    placed = (
        P(("row", "col"), None),
        P(),
        P(),
        P(("row", "col")),
        P(("row", "col"), None),
        P("row", "col", None),
        P("row", "col", None),
        P("row", "col"),
        P("row", "col", None, None, None),
    )
    return jax.shard_map(
        functools.partial(shards, mesh.shape["row"], mesh.shape["col"]),
        mesh=mesh,
        in_specs=placed,
        out_specs=(P(("row", "col"), None), P(("row", "col"), None), P(), P()),
        check_vma=False,
    )
```

time: 48.3 us -> 48.1 us (level)
  Pallas kernels: 39.9 us -> 46.7 us
  local copies, waits for them, and re-layouts: 6.74 us -> 0 us
    pallas_call x1 -> x2, Pallas kernels: 39.9 us -> 46.7 us  [the longest x1 39.6 us: shards(): pl.pallas_call(functools.partial(layer_kernel, n_row, n_col, slots, halve...]
    unnamed x20 -> x0, local copies, waits for them, and re-layouts: 6.74 us -> none
where the time goes in v2:
time: 48.1 us; the launch traced here: 48 us
  Pallas kernels  46.7 us (97%)
  between operations  1.29 us (3%)
    pallas_call x1, Pallas kernels, shards(): pl.pallas_call(functools.partial(layer_kernel, n_row, n_col, slots, halve...  39.6 us
    pallas_call x1, Pallas kernels, shards(): pl.pallas_call(functools.partial(finish_kernel, 4), out_shape=shapes, in_...  7.11 us

profile of v2, /device:TPU:0, one launch (start us, length us, event | category | flops | bytes accessed | tf_op | source)
XLA Modules:
  0.0 48.0 jit_solution(4518935995479791750)
XLA Ops:
  1.3 39.6 %shard_map.120 = (bf16[256,128]{1,0:T(8,128)(2,1)}, bf16[256,128]{1,0:T(8,128)(2,1)}, f32[128,128]{1,0:T(8,128)}, f32[1,128]{1,0:T(1,128)}) custom-call(s32[8]{0:T(128)} %bitcast.10, s32[8]{0:T(128)} %bitcast.11, s32[1]{0:T(128)} %bitcast.7.count_hbm, bf16[256,128]{1,0:T(8,128)(2,1)} %features_hbm.1, bf16[128,128]{1,0:T(8,128)(2,1)} %weight_hbm.1, ...), custom_call_target="tpu_custom_call" | custom-call | tf_op jit(solution)/shard_map/pallas_call | solution.py:270
  40.9 7.1 %shard_map.121 = (bf16[256,128]{1,0:T(8,128)(2,1)}, bf16[256,128]{1,0:T(8,128)(2,1)}, f32[128,128]{1,0:T(8,128)}, f32[1,128]{1,0:T(1,128)}) custom-call(bf16[256,128]{1,0:T(8,128)(2,1)} %get-tuple-element.12.refs_0_, bf16[256,128]{1,0:T(8,128)(2,1)} %get-tuple-element.13.refs_1_, f32[128,128]{1,0:T(8,128)} %get-tuple-element.14.refs_2_, ...), custom_call_target="tpu_custom_call" | custom-call | tf_op jit(solution)/shard_map/pallas_call | solution.py:311

commit v3 on v2

--- a/solution.py
+++ b/solution.py
@@ -24,7 +24,7 @@
     tiles_hbm,
     act_hbm, fgrad_hbm, wgrad_hbm, bgrad_hbm,
     act_ref, fgrad_ref, wgrad_ref, bgrad_ref, store_sem, rows_ref, cols_ref, count_ref, features, weight, bias, scale_ref, cotangent,
-    tiles, tiles_t, terms, out_row, out_col, in_row, in_col,
+    tiles, tiles_t, terms, out_row, out_col, in_row, in_col, pair,
     w_part, w_in, w_cross, w_all, load_sem, send_sem, recv_sem, *blocks,
 ):
     r = lax.axis_index("row")
@@ -44,6 +44,15 @@
 
     row_peers = [lax.rem(r + k, n_row) for k in range(n_row)]
     col_peers = [lax.rem(c + k, n_col) for k in range(n_col)]
+    chips = n_row // 2
+    sibling = r + 1 - 2 * lax.rem(r, 2)
+    mates = [lax.rem(r + 2 * k, n_row) for k in range(chips)]
+    mate_siblings = [lax.rem(sibling + 2 * k, n_row) for k in range(chips)]
+    line = n_col == 4
+    near = c + 1 - 2 * lax.rem(c, 2)
+    cross = 2 - c // 2
+    far = 3 * (1 - c // 2)
+    middle = lax.rem((c + 1) // 2, 2)
 
     barrier = pltpu.get_barrier_semaphore()
     for peer in row_peers[1:]:
@@ -52,48 +61,52 @@
         pl.semaphore_signal(barrier, inc=1, device_id=(r, peer), device_id_type=MESH)
 
     sent = []
+    sent_by_middle = []
+    sent_by_ends = []
+    stores = []
 
     def store(n, src, dst):
         copy = pltpu.make_async_copy(src, dst, store_sem.at[n])
         copy.start()
         stores.append(copy)
 
-    stores = []
-
-    def send_along_row(stage, k, src, dst):
+    def to_row(stage, n, peer, src, dst, slot):
         copy = pltpu.make_async_remote_copy(
-            src_ref=src, dst_ref=dst.at[r],
-            send_sem=send_sem.at[stage, k], recv_sem=recv_sem.at[stage, r],
-            device_id=(row_peers[k], c), device_id_type=MESH)
+            src_ref=src, dst_ref=dst.at[slot],
+            send_sem=send_sem.at[stage, n], recv_sem=recv_sem.at[stage, slot],
+            device_id=(peer, c), device_id_type=MESH)
         copy.start()
         sent.append(copy)
 
-    def send_along_col(stage, k, src, dst):
+    def to_col(stage, n, peer, src, dst, slot, when=None):
         copy = pltpu.make_async_remote_copy(
-            src_ref=src, dst_ref=dst.at[c],
-            send_sem=send_sem.at[stage, n_row + k], recv_sem=recv_sem.at[stage, n_row + c],
-            device_id=(r, col_peers[k]), device_id_type=MESH)
-        copy.start()
-        sent.append(copy)
-
-    def wait_row(stage, dst, k):
-        peer = row_peers[k]
+            src_ref=src, dst_ref=dst.at[slot],
+            send_sem=send_sem.at[stage, n_row + n], recv_sem=recv_sem.at[stage, n_row + slot],
+            device_id=(r, peer), device_id_type=MESH)
+        if when is None:
+            copy.start()
+            sent.append(copy)
+        else:
+            pl.when(when)(copy.start)
+            sent_by_middle.append(copy)
+
+    def wait_row(stage, dst, slot):
         pltpu.make_async_remote_copy(
-            src_ref=dst.at[peer], dst_ref=dst.at[peer],
-            send_sem=send_sem.at[stage, k], recv_sem=recv_sem.at[stage, peer],
-            device_id=(peer, c), device_id_type=MESH).wait_recv()
-
-    def wait_col(stage, dst, k):
-        peer = col_peers[k]
+            src_ref=dst.at[slot], dst_ref=dst.at[slot],
+            send_sem=send_sem.at[stage, 0], recv_sem=recv_sem.at[stage, slot],
+            device_id=(sibling, c), device_id_type=MESH).wait_recv()
+
+    def wait_col(stage, dst, slot):
         pltpu.make_async_remote_copy(
-            src_ref=dst.at[peer], dst_ref=dst.at[peer],
-            send_sem=send_sem.at[stage, n_row + k], recv_sem=recv_sem.at[stage, n_row + peer],
-            device_id=(r, peer), device_id_type=MESH).wait_recv()
+            src_ref=dst.at[slot], dst_ref=dst.at[slot],
+            send_sem=send_sem.at[stage, 0], recv_sem=recv_sem.at[stage, n_row + slot],
+            device_id=(sibling, c), device_id_type=MESH).wait_recv()
 
     x_row = blocks[: 2 * halves]
     x_col = blocks[2 * halves:]
     spread_at = 2 * halves
-    sum_at = 4 * halves
+    pair_at = 4 * halves
+    sum_at = 6 * halves
 
     def gather(step, block):
         xr, xc = x_row[step], x_col[step]
@@ -101,48 +114,118 @@
         xc[r] = block
         if step == 0:
             pl.semaphore_wait(barrier, n_row + n_col - 2)
-        for k in range(1, max(n_row, n_col)):
-            if k < n_col:
-                send_along_col(step, k, xr.at[c], xr)
-            if k < n_row:
-                send_along_row(step, k, xc.at[r], xc)
+        if line:
+            to_col(step, 0, cross, xr.at[c], xr, c)
+            to_col(step, 1, near, xr.at[c], xr, c)
+            to_col(step, 2, far, xr.at[c], xr, c, when=middle == 1)
+        else:
+            for k in range(1, n_col):
+                to_col(step, k, col_peers[k], xr.at[c], xr, c)
+        for k in range(1, chips):
+            to_row(step, k, mates[k], xc.at[r], xc, r)
+        to_row(step, chips, sibling, xc.at[r], xc, r)
+
+    def forward(step):
+        xr, xc = x_row[step], x_col[step]
+        for k in range(1, chips):
+            wait_row(step, xc, mates[k])
+            to_row(step, chips + k, sibling, xc.at[mates[k]], xc, mates[k])
+        if line:
+            @pl.when(middle == 1)
+            def _():
+                wait_col(step, xr, far)
+            to_col(step, 3, near, xr.at[far], xr, far, when=middle == 1)
 
     def partial(at, index, weights):
         total = None
         for t in range(slots):
             term = terms[t] * jnp.where(at[t] == index, weights[t], 0.0)
             total = term if total is None else total + term
-        return total.astype(BF16)
+        return total
 
     def spread(step, row_at, col_at, weights):
         xr, xc = x_row[step], x_col[step]
-        for k in range(1, n_col):
-            wait_col(step, xr, k)
+        row_out, col_out, row_in, col_in = (
+            ref.at[step] for ref in (out_row, out_col, in_row, in_col))
+        stage = spread_at + step
+        wait_row(step, xc, sibling)
+        for k in range(1, chips):
+            wait_row(step, xc, mate_siblings[k])
+        for t in range(slots):
+            terms[t] = dot(xc[col_at[t]], tiles_t[t])
+        if line:
+            relayed = pltpu.make_async_remote_copy(
+                src_ref=row_out.at[2], dst_ref=row_in.at[n_col],
+                send_sem=send_sem.at[stage, n_row + 2], recv_sem=recv_sem.at[stage, n_row + n_col],
+                device_id=(r, near), device_id_type=MESH)
+
+            @pl.when(middle == 0)
+            def _():
+                row_out[2] = partial(row_at, far, weights).astype(BF16)
+                row_in[far] = jnp.zeros_like(row_in[far])
+                relayed.start()
+            sent_by_ends.append(relayed)
+            row_out[0] = partial(row_at, cross, weights).astype(BF16)
+            to_col(stage, 0, cross, row_out.at[0], row_in, c)
+            row_out[1] = partial(row_at, near, weights).astype(BF16)
+            to_col(stage, 1, near, row_out.at[1], row_in, c)
+            row_in[c] = partial(row_at, c, weights).astype(BF16)
+
+            @pl.when(middle == 1)
+            def _():
+                wait_col(stage, row_in, n_col)
+                row_out[2] = (partial(row_at, far, weights) + row_in[n_col].astype(F32)).astype(BF16)
+            to_col(stage, 2, far, row_out.at[2], row_in, c, when=middle == 1)
+        else:
+            for k in range(1, n_col):
+                row_out[k - 1] = partial(row_at, col_peers[k], weights).astype(BF16)
+                to_col(stage, k, col_peers[k], row_out.at[k - 1], row_in, c)
+            row_in[c] = partial(row_at, c, weights).astype(BF16)
+
+        if line:
+            wait_col(step, xr, near)
+            wait_col(step, xr, cross)
+
+            @pl.when(middle == 0)
+            def _():
+                wait_col(step, xr, far)
+        else:
+            for k in range(1, n_col):
+                wait_col(step, xr, col_peers[k])
         for t in range(slots):
             terms[t] = dot(xr[row_at[t]], tiles[t])
-        for k in range(1, n_row):
-            out_col[step, k] = partial(col_at, row_peers[k], weights)
-            send_along_row(spread_at + step, k, out_col.at[step, k], in_col.at[step])
-        in_col[step, r] = partial(col_at, r, weights)
-        for k in range(1, n_row):
-            wait_row(step, xc, k)
-        for t in range(slots):
-            terms[t] = dot(xc[col_at[t]], tiles_t[t])
-        for k in range(1, n_col):
-            out_row[step, k] = partial(row_at, col_peers[k], weights)
-            send_along_col(spread_at + step, k, out_row.at[step, k], in_row.at[step])
-        in_row[step, c] = partial(row_at, c, weights)
+        for k in range(1, chips):
+            col_out[k] = partial(col_at, mate_siblings[k], weights).astype(BF16)
+            to_row(pair_at + step, k, sibling, col_out.at[k], pair.at[step], k)
+        col_out[0] = partial(col_at, sibling, weights).astype(BF16)
+        to_row(stage, 0, sibling, col_out.at[0], col_in, chips)
+        col_in[0] = partial(col_at, r, weights).astype(BF16)
+        for k in range(1, chips):
+            mine = partial(col_at, mates[k], weights)
+            wait_row(pair_at + step, pair.at[step], k)
+            col_out[chips + k] = (mine + pair[step, k].astype(F32)).astype(BF16)
+            to_row(stage, k, mates[k], col_out.at[chips + k], col_in, k)
 
     def collect(step, own):
-        for k in range(1, n_row):
-            wait_row(spread_at + step, in_col.at[step], k)
-        for k in range(1, n_col):
-            wait_col(spread_at + step, in_row.at[step], k)
+        row_in, col_in = in_row.at[step], in_col.at[step]
+        stage = spread_at + step
+        if line:
+            wait_col(stage, row_in, near)
+            wait_col(stage, row_in, cross)
+
+            @pl.when(middle == 1)
+            def _():
+                wait_col(stage, row_in, far)
+        else:
+            for k in range(1, n_col):
+                wait_col(stage, row_in, col_peers[k])
         total = own.astype(F32)
-        for k in range(n_row):
-            total = total + in_col[step, k].astype(F32)
         for k in range(n_col):
-            total = total + in_row[step, k].astype(F32)
+            total = total + row_in[k].astype(F32)
+        for k in range(1, chips + 1):
+            wait_row(stage, col_in, k)
+        for k in range(chips + 1):
+            total = total + col_in[k].astype(F32)
         return total
 
     for load in loads[:2]:
@@ -167,6 +250,7 @@
     for t in range(slots):
         tiles_t[t] = tiles[t].T
     for h in range(halves):
+        forward(h)
         spread(h, row_at, col_at, weights)
     mixed = jnp.concatenate(
         [collect(h, scaled[h * part:(h + 1) * part]) for h in range(halves)], axis=0)
@@ -194,29 +278,31 @@
         w_part[k, :chunk, :] = local[k * chunk:(k + 1) * chunk]
         w_part[k, chunk:, :] = jnp.broadcast_to(local_bias, (8, width))
     for k in range(1, n_row):
-        send_along_row(sum_at, k, w_part.at[row_peers[k]], w_in)
+        to_row(sum_at, k, row_peers[k], w_part.at[row_peers[k]], w_in, r)
     w_in[r] = w_part[r]
     act_ref[...] = jnp.concatenate(acts, axis=0).T.astype(BF16)
     store(0, act_ref, act_hbm)
     for h in range(halves - 1):
+        forward(halves + h)
         spread(halves + h, row_at, col_at, weights)
     for k in range(1, n_row):
-        wait_row(sum_at, w_in, k)
+        wait_row(sum_at, w_in, row_peers[k])
     summed = w_in[0]
     for k in range(1, n_row):
         summed = summed + w_in[k]
     w_cross[c] = summed
     for k in range(1, n_col):
-        send_along_col(sum_at, k, w_cross.at[c], w_cross)
+        to_col(sum_at, k, col_peers[k], w_cross.at[c], w_cross, c)
+    forward(2 * halves - 1)
     spread(2 * halves - 1, row_at, col_at, weights)
     for k in range(1, n_col):
-        wait_col(sum_at, w_cross, k)
+        wait_col(sum_at, w_cross, col_peers[k])
     summed = w_cross[0]
     for k in range(1, n_col):
         summed = summed + w_cross[k]
     w_all[r] = summed
     for k in range(1, n_row):
-        send_along_row(sum_at + 1, k, w_all.at[r], w_all)
+        to_row(sum_at + 1, k, row_peers[k], w_all.at[r], w_all, r)
     bgrad_ref[...] = summed[chunk:chunk + 1]
     store(3, bgrad_ref, bgrad_hbm)
 
@@ -228,24 +314,37 @@
     fgrad_ref[...] = fgrad_t.T.astype(BF16)
     store(1, fgrad_ref, fgrad_hbm)
     for k in range(1, n_row):
-        wait_row(sum_at + 1, w_all, k)
+        wait_row(sum_at + 1, w_all, row_peers[k])
     for k in range(n_row):
         wgrad_ref[k * chunk:(k + 1) * chunk, :] = w_all[k, :chunk, :]
     store(2, wgrad_ref, wgrad_hbm)
     for copy in sent:
         copy.wait_send()
+
+    @pl.when(middle == 1)
+    def _():
+        for copy in sent_by_middle:
+            copy.wait_send()
+
+    @pl.when(middle == 0)
+    def _():
+        for copy in sent_by_ends:
+            copy.wait_send()
     for copy in stores:
         copy.wait()
 
 
 def finish_kernel(count, *refs):
+    sources, results, held = (refs[n * count:(n + 1) * count] for n in range(3))
     sem = refs[-1]
-    copies = [
-        pltpu.make_async_copy(refs[n], refs[count + n], sem.at[n]) for n in range(count)
-    ]
-    for copy in copies:
-        copy.start()
-    for copy in copies:
+    fetches = [pltpu.make_async_copy(sources[n], held[n], sem.at[0, n]) for n in range(count)]
+    stores = [pltpu.make_async_copy(held[n], results[n], sem.at[1, n]) for n in range(count)]
+    for fetch in fetches:
+        fetch.start()
+    for n in range(count):
+        fetches[n].wait()
+        stores[n].start()
+    for copy in stores:
         copy.wait()
 
 
@@ -288,15 +387,16 @@
             pltpu.VMEM((slots, part, BLOCK), F32),
             pltpu.VMEM((2 * halves, n_col, part, BLOCK), BF16),
             pltpu.VMEM((2 * halves, n_row, part, BLOCK), BF16),
-            pltpu.VMEM((2 * halves, n_col, part, BLOCK), BF16),
-            pltpu.VMEM((2 * halves, n_row, part, BLOCK), BF16),
+            pltpu.VMEM((2 * halves, n_col + 1, part, BLOCK), BF16),
+            pltpu.VMEM((2 * halves, n_row // 2 + 1, part, BLOCK), BF16),
+            pltpu.VMEM((2 * halves, n_row // 2, part, BLOCK), BF16),
             pltpu.VMEM((n_row, chunk + 8, width), F32),
             pltpu.VMEM((n_row, chunk + 8, width), F32),
             pltpu.VMEM((n_col, chunk + 8, width), F32),
             pltpu.VMEM((n_row, chunk + 8, width), F32),
             pltpu.SemaphoreType.DMA((9,)),
-            pltpu.SemaphoreType.DMA((4 * halves + 2, peers)),
-            pltpu.SemaphoreType.DMA((4 * halves + 2, peers)),
+            pltpu.SemaphoreType.DMA((6 * halves + 2, peers + 1)),
+            pltpu.SemaphoreType.DMA((6 * halves + 2, peers + 1)),
         ]
         + [pltpu.VMEM((n_col, part, BLOCK), BF16)] * (2 * halves)
         + [pltpu.VMEM((n_row, part, BLOCK), BF16)] * (2 * halves),
@@ -313,7 +413,8 @@
         out_shape=shapes,
         in_specs=[pl.BlockSpec(memory_space=pl.ANY)] * 4,
         out_specs=(hbm,) * 4,
-        scratch_shapes=[pltpu.SemaphoreType.DMA((4,))],
+        scratch_shapes=[pltpu.VMEM(shape.shape, shape.dtype) for shape in shapes]
+        + [pltpu.SemaphoreType.DMA((2, 4))],
         compiler_params=pltpu.CompilerParams(vmem_limit_bytes=VMEM_LIMIT),
     )(*results)
     return act, fgrad, wgrad, bgrad.reshape(width)

time: 48.1 us -> 48.3 us (level)
    pallas_call x1, Pallas kernels: 39.6 us -> 45.3 us  [shards(): pl.pallas_call(functools.partial(layer_kernel, n_row, n_col, slots, halve...]
    pallas_call x1, Pallas kernels: 7.11 us -> 1.6 us  [shards(): pl.pallas_call(functools.partial(finish_kernel, 4), out_shape=shapes, in_...]
where the time goes in v3:
time: 48.3 us; the launch traced here: 48.2 us
  Pallas kernels  46.9 us (97%)
  between operations  1.29 us (3%)
    pallas_call x1, Pallas kernels, shards(): pl.pallas_call(functools.partial(layer_kernel, n_row, n_col, slots, halve...  45.3 us
    pallas_call x1, Pallas kernels, shards(): pl.pallas_call(functools.partial(finish_kernel, 4), out_shape=shapes, in_...  1.6 us

profile of v3, /device:TPU:0, one launch (start us, length us, event | category | flops | bytes accessed | tf_op | source)
XLA Modules:
  0.0 48.2 jit_solution(11724168125731468854)
XLA Ops:
  1.3 45.3 %shard_map.120 = (bf16[256,128]{1,0:T(8,128)(2,1)}, bf16[256,128]{1,0:T(8,128)(2,1)}, f32[128,128]{1,0:T(8,128)}, f32[1,128]{1,0:T(1,128)}) custom-call(s32[8]{0:T(128)} %bitcast.10, s32[8]{0:T(128)} %bitcast.11, s32[1]{0:T(128)} %bitcast.7.count_hbm, bf16[256,128]{1,0:T(8,128)(2,1)} %features_hbm.1, bf16[128,128]{1,0:T(8,128)(2,1)} %weight_hbm.1, ...), custom_call_target="tpu_custom_call" | custom-call | tf_op jit(solution)/shard_map/pallas_call | solution.py:369
  46.5 1.6 %shard_map.121 = (bf16[256,128]{1,0:T(8,128)(2,1)}, bf16[256,128]{1,0:T(8,128)(2,1)}, f32[128,128]{1,0:T(8,128)}, f32[1,128]{1,0:T(1,128)}) custom-call(bf16[256,128]{1,0:T(8,128)(2,1)} %get-tuple-element.12.refs_0_, bf16[256,128]{1,0:T(8,128)(2,1)} %get-tuple-element.13.refs_1_, f32[128,128]{1,0:T(8,128)} %get-tuple-element.14.refs_2_, ...), custom_call_target="tpu_custom_call" | custom-call | tf_op jit(solution)/shard_map/pallas_call | solution.py:411

commit v4 on v2

v4 whole, which is shorter than its diff:
```python
import functools

import jax
import jax.numpy as jnp
from jax import lax
from jax.experimental import pallas as pl
from jax.experimental.pallas import tpu as pltpu
from jax.sharding import PartitionSpec as P

BLOCK = 256
VMEM_LIMIT = 60 * 1024 * 1024
MESH = pl.DeviceIdType.MESH
F32 = jnp.float32
BF16 = jnp.bfloat16


def dot(a, b, dims=((1,), (0,))):
    return lax.dot_general(a, b, (dims, ((), ())), preferred_element_type=F32)


def layer_kernel(
    n_row, n_col, slots,
    rows_hbm, cols_hbm, count_hbm, features_hbm, weight_hbm, bias_hbm, scale_hbm, cotangent_hbm,
    tiles_hbm,
    act_hbm, fgrad_hbm, wgrad_hbm, bgrad_hbm,
    act_ref, fgrad_ref, wgrad_ref, bgrad_ref, store_sem, rows_ref, cols_ref, count_ref,
    features, weight, bias, scale_ref, cotangent,
    tiles, tiles_t, terms, out_row, out_col, in_row, in_col,
    w_part, w_in, w_cross, w_all, load_sem, send_row_sem, send_col_sem, recv_row_sem, recv_col_sem,
    x_row0, x_row1, x_col0, x_col1,
):
    r = lax.axis_index("row")
    c = lax.axis_index("col")
    width = features.shape[1]
    chunk = width // n_row

    pairs = (
        (features_hbm, features), (scale_hbm, scale_ref), (rows_hbm, rows_ref), (cols_hbm, cols_ref),
        (count_hbm, count_ref), (tiles_hbm, tiles), (weight_hbm, weight), (bias_hbm, bias),
        (cotangent_hbm, cotangent),
    )
    loads = [pltpu.make_async_copy(src, dst, load_sem.at[n]) for n, (src, dst) in enumerate(pairs)]
    for load in loads:
        load.start()

    def row_peer(k):
        return lax.rem(r + k, n_row)

    def col_peer(k):
        return lax.rem(c + k, n_col)

    def each(first, last, body):
        def step(k, carry):
            body(k)
            return carry
        lax.fori_loop(first, last, step, 0)

    barrier = pltpu.get_barrier_semaphore()
    each(1, n_row, lambda k: pl.semaphore_signal(
        barrier, inc=1, device_id=(row_peer(k), c), device_id_type=MESH))
    each(1, n_col, lambda k: pl.semaphore_signal(
        barrier, inc=1, device_id=(r, col_peer(k)), device_id_type=MESH))

    def row_copy(stage, k, src, dst):
        return pltpu.make_async_remote_copy(
            src_ref=src, dst_ref=dst, send_sem=send_row_sem.at[stage], recv_sem=recv_row_sem.at[stage],
            device_id=(row_peer(k), c), device_id_type=MESH)

    def col_copy(stage, k, src, dst):
        return pltpu.make_async_remote_copy(
            src_ref=src, dst_ref=dst, send_sem=send_col_sem.at[stage], recv_sem=recv_col_sem.at[stage],
            device_id=(r, col_peer(k)), device_id_type=MESH)

    def row_all(stage, buffer):
        whole = buffer.at[pl.ds(0, n_row - 1)]
        return row_copy(stage, 1, whole, whole)

    def col_all(stage, buffer):
        whole = buffer.at[pl.ds(0, n_col - 1)]
        return col_copy(stage, 1, whole, whole)

    x_row = (x_row0, x_row1)
    x_col = (x_col0, x_col1)

    def store(n, src, dst):
        copy = pltpu.make_async_copy(src, dst, store_sem.at[n])
        copy.start()
        stores.append(copy)

    stores = []

    def gather(phase, block):
        xr, xc = x_row[phase], x_col[phase]
        xr[c] = block
        xc[r] = block
        if phase == 0:
            pl.semaphore_wait(barrier, n_row + n_col - 2)
        each(1, n_col, lambda k: col_copy(phase, k, xr.at[c], xr.at[c]).start())
        each(1, n_row, lambda k: row_copy(phase, k, xc.at[r], xc.at[r]).start())

    def partial(at, index):
        total = None
        for t in range(slots):
            term = terms[t] * jnp.where(at[t] == index, weights[t], 0.0)
            total = term if total is None else total + term
        return total.astype(BF16)

    def spread(phase, between=None):
        xr, xc = x_row[phase], x_col[phase]
        stage = 2 + phase
        col_all(phase, xr).wait_recv()
        for t in range(slots):
            terms[t] = dot(xr[row_at[t]], tiles[t])

        def to_row(k):
            out_col[phase, k] = partial(col_at, row_peer(k))
            row_copy(stage, k, out_col.at[phase, k], in_col.at[phase, r]).start()

        each(1, n_row, to_row)
        in_col[phase, r] = partial(col_at, r)
        if between is not None:
            between()
        row_all(phase, xc).wait_recv()
        for t in range(slots):
            terms[t] = dot(xc[col_at[t]], tiles_t[t])

        def to_col(k):
            out_row[phase, k] = partial(row_at, col_peer(k))
            col_copy(stage, k, out_row.at[phase, k], in_row.at[phase, c]).start()

        each(1, n_col, to_col)
        in_row[phase, c] = partial(row_at, c)

    def collect(phase, own):
        total = own.astype(F32)
        row_all(2 + phase, in_col.at[phase]).wait_recv()
        for k in range(n_row):
            total = total + in_col[phase, k].astype(F32)
        col_all(2 + phase, in_row.at[phase]).wait_recv()
        for k in range(n_col):
            total = total + in_row[phase, k].astype(F32)
        return total

    for load in loads[:2]:
        load.wait()
    scale = scale_ref[...]
    scaled = (scale * features[...].astype(F32).T).astype(BF16)
    gather(0, scaled)
    for load in loads[2:]:
        load.wait()
    row_at = [rows_ref[t] for t in range(slots)]
    col_at = [cols_ref[t] for t in range(slots)]
    count = count_ref[0]
    weights = [
        jnp.where(
            t < count,
            jnp.where(r * n_col + row_at[t] == col_at[t] * n_col + c, 0.5, 1.0),
            0.0,
        ).astype(F32)
        for t in range(slots)
    ]

    def transpose(t):
        tiles_t[t] = tiles[t].T

    each(0, slots, transpose)
    spread(0)
    weight_t = weight[...].T
    bias_t = jnp.broadcast_to(bias[...], (BLOCK, width)).T
    cotangent_t = cotangent[...].astype(F32).T
    mixed = collect(0, scaled)
    high = mixed.astype(BF16)
    low = (mixed - high.astype(F32)).astype(BF16)
    product = dot(weight_t, high) + dot(weight_t, low)
    preact = scale * product + bias_t
    sig = 1.0 / (1.0 + jnp.exp(-preact))
    delta = cotangent_t * sig * (1.0 + preact * (1.0 - sig))
    scaled_delta = (scale * delta).astype(BF16)
    gather(1, scaled_delta)

    local = dot(high, scaled_delta, ((1,), (1,)))
    local_bias = jnp.sum(delta.T, axis=0, keepdims=True)
    for k in range(n_row):
        w_part[k, :chunk, :] = local[k * chunk:(k + 1) * chunk]
        w_part[k, chunk:, :] = jnp.broadcast_to(local_bias, (8, width))
    each(1, n_row, lambda k: row_copy(4, k, w_part.at[row_peer(k)], w_in.at[r]).start())
    w_in[r] = w_part[r]
    act_ref[...] = (preact * sig).T.astype(BF16)
    store(0, act_ref, act_hbm)

    def sum_over_row():
        row_all(4, w_in).wait_recv()
        summed = w_in[0]
        for k in range(1, n_row):
            summed = summed + w_in[k]
        w_cross[c] = summed
        each(1, n_col, lambda k: col_copy(4, k, w_cross.at[c], w_cross.at[c]).start())

    spread(1, sum_over_row)
    col_all(4, w_cross).wait_recv()
    summed = w_cross[0]
    for k in range(1, n_col):
        summed = summed + w_cross[k]
    w_all[r] = summed
    each(1, n_row, lambda k: row_copy(5, k, w_all.at[r], w_all.at[r]).start())
    bgrad_ref[...] = summed[chunk:chunk + 1]
    store(3, bgrad_ref, bgrad_hbm)

    proj_grad = (scale * collect(1, scaled_delta)).astype(BF16)
    fgrad_ref[...] = dot(weight[...], proj_grad).T.astype(BF16)
    store(1, fgrad_ref, fgrad_hbm)
    row_all(5, w_all).wait_recv()
    for k in range(n_row):
        wgrad_ref[k * chunk:(k + 1) * chunk, :] = w_all[k, :chunk, :]
    store(2, wgrad_ref, wgrad_hbm)
    for stage in range(6):
        row_all(stage, x_col0 if stage < 4 else w_in).wait_send()
    for stage in range(5):
        col_all(stage, x_row0 if stage < 4 else w_cross).wait_send()
    for copy in stores:
        copy.wait()


def finish_kernel(count, *refs):
    sources, results, held = (refs[n * count:(n + 1) * count] for n in range(3))
    sem = refs[-1]
    fetches = [pltpu.make_async_copy(sources[n], held[n], sem.at[0, n]) for n in range(count)]
    stores = [pltpu.make_async_copy(held[n], results[n], sem.at[1, n]) for n in range(count)]
    for fetch in fetches:
        fetch.start()
    for n in range(count):
        fetches[n].wait()
        stores[n].start()
    for copy in stores:
        copy.wait()


def shards(
    n_row, n_col,
    features, weight, bias, node_scale, cotangent, tile_row, tile_col, tile_count, tile_values
):
    width = features.shape[1]
    slots = tile_row.shape[-1]
    assert features.shape[0] == BLOCK
    chunk = width // n_row
    hbm = pl.BlockSpec(memory_space=pltpu.HBM)
    shapes = (
        jax.ShapeDtypeStruct((BLOCK, width), BF16),
        jax.ShapeDtypeStruct((BLOCK, width), BF16),
        jax.ShapeDtypeStruct((width, width), F32),
        jax.ShapeDtypeStruct((1, width), F32),
    )
    results = pl.pallas_call(
        functools.partial(layer_kernel, n_row, n_col, slots),
        out_shape=shapes,
        in_specs=[hbm] * 9,
        out_specs=(hbm,) * 4,
        scratch_shapes=[pltpu.VMEM(shape.shape, shape.dtype) for shape in shapes]
        + [
            pltpu.SemaphoreType.DMA((4,)),
            pltpu.SMEM((slots,), jnp.int32),
            pltpu.SMEM((slots,), jnp.int32),
            pltpu.SMEM((1,), jnp.int32),
            pltpu.VMEM((BLOCK, width), BF16),
            pltpu.VMEM((width, width), BF16),
            pltpu.VMEM((1, width), F32),
            pltpu.VMEM((1, BLOCK), F32),
            pltpu.VMEM((BLOCK, width), BF16),
            pltpu.VMEM((slots, BLOCK, BLOCK), BF16),
            pltpu.VMEM((slots, BLOCK, BLOCK), BF16),
            pltpu.VMEM((slots, width, BLOCK), F32),
            pltpu.VMEM((2, n_col, width, BLOCK), BF16),
            pltpu.VMEM((2, n_row, width, BLOCK), BF16),
            pltpu.VMEM((2, n_col, width, BLOCK), BF16),
            pltpu.VMEM((2, n_row, width, BLOCK), BF16),
            pltpu.VMEM((n_row, chunk + 8, width), F32),
            pltpu.VMEM((n_row, chunk + 8, width), F32),
            pltpu.VMEM((n_col, chunk + 8, width), F32),
            pltpu.VMEM((n_row, chunk + 8, width), F32),
            pltpu.SemaphoreType.DMA((9,)),
            pltpu.SemaphoreType.DMA((6,)),
            pltpu.SemaphoreType.DMA((5,)),
            pltpu.SemaphoreType.DMA((6,)),
            pltpu.SemaphoreType.DMA((5,)),
            pltpu.VMEM((n_col, width, BLOCK), BF16),
            pltpu.VMEM((n_col, width, BLOCK), BF16),
            pltpu.VMEM((n_row, width, BLOCK), BF16),
            pltpu.VMEM((n_row, width, BLOCK), BF16),
        ],
        compiler_params=pltpu.CompilerParams(
            collective_id=0, has_side_effects=True, vmem_limit_bytes=VMEM_LIMIT
        ),
    )(
        tile_row.reshape(slots), tile_col.reshape(slots), tile_count.reshape(1),
        features, weight, bias.reshape(1, width), node_scale.reshape(1, BLOCK), cotangent,
        tile_values.reshape(slots, BLOCK, BLOCK),
    )
    act, fgrad, wgrad, bgrad = pl.pallas_call(
        functools.partial(finish_kernel, 4),
        out_shape=shapes,
        in_specs=[pl.BlockSpec(memory_space=pl.ANY)] * 4,
        out_specs=(hbm,) * 4,
        scratch_shapes=[pltpu.VMEM(shape.shape, shape.dtype) for shape in shapes]
        + [pltpu.SemaphoreType.DMA((2, 4))],
        compiler_params=pltpu.CompilerParams(vmem_limit_bytes=VMEM_LIMIT),
    )(*results)
    return act, fgrad, wgrad, bgrad.reshape(width)


def solution(mesh):
    placed = (
        P(("row", "col"), None),
        P(),
        P(),
        P(("row", "col")),
        P(("row", "col"), None),
        P("row", "col", None),
        P("row", "col", None),
        P("row", "col"),
        P("row", "col", None, None, None),
    )
    return jax.shard_map(
        functools.partial(shards, mesh.shape["row"], mesh.shape["col"]),
        mesh=mesh,
        in_specs=placed,
        out_specs=(P(("row", "col"), None), P(("row", "col"), None), P(), P()),
        check_vma=False,
    )
```

time: 48.1 us -> 41.3 us (0.86)
  Pallas kernels: 46.7 us -> 39.8 us
    pallas_call x1, Pallas kernels: 7.11 us -> 1.6 us  [shards(): pl.pallas_call(functools.partial(finish_kernel, 4), out_shape=shapes, in_...]
    pallas_call x1, Pallas kernels: 39.6 us -> 38.2 us  [shards(): pl.pallas_call(functools.partial(layer_kernel, n_row, n_col, slots), out_...]
where the time goes in v4:
time: 41.3 us; the launch traced here: 41.1 us
  Pallas kernels  39.8 us (96%)
  between operations  1.29 us (3%)
    pallas_call x1, Pallas kernels, shards(): pl.pallas_call(functools.partial(layer_kernel, n_row, n_col, slots), out_...  38.2 us
    pallas_call x1, Pallas kernels, shards(): pl.pallas_call(functools.partial(finish_kernel, 4), out_shape=shapes, in_...  1.6 us

profile of v4, /device:TPU:0, one launch (start us, length us, event | category | flops | bytes accessed | tf_op | source)
XLA Modules:
  0.0 41.1 jit_solution(16550919700187749965)
XLA Ops:
  1.3 38.2 %shard_map.120 = (bf16[256,128]{1,0:T(8,128)(2,1)}, bf16[256,128]{1,0:T(8,128)(2,1)}, f32[128,128]{1,0:T(8,128)}, f32[1,128]{1,0:T(1,128)}) custom-call(s32[8]{0:T(128)} %bitcast.10, s32[8]{0:T(128)} %bitcast.11, s32[1]{0:T(128)} %bitcast.7.count_hbm, bf16[256,128]{1,0:T(8,128)(2,1)} %features_hbm.1, bf16[128,128]{1,0:T(8,128)(2,1)} %weight_hbm.1, ...), custom_call_target="tpu_custom_call" | custom-call | tf_op jit(solution)/shard_map/pallas_call | solution.py:253
  39.5 1.6 %shard_map.121 = (bf16[256,128]{1,0:T(8,128)(2,1)}, bf16[256,128]{1,0:T(8,128)(2,1)}, f32[128,128]{1,0:T(8,128)}, f32[1,128]{1,0:T(1,128)}) custom-call(bf16[256,128]{1,0:T(8,128)(2,1)} %get-tuple-element.12.refs_0_, bf16[256,128]{1,0:T(8,128)(2,1)} %get-tuple-element.13.refs_1_, f32[128,128]{1,0:T(8,128)} %get-tuple-element.14.refs_2_, ...), custom_call_target="tpu_custom_call" | custom-call | tf_op jit(solution)/shard_map/pallas_call | solution.py:298

commit v5 on v4

--- a/solution.py
+++ b/solution.py
@@ -25,7 +25,7 @@
     act_hbm, fgrad_hbm, wgrad_hbm, bgrad_hbm,
     act_ref, fgrad_ref, wgrad_ref, bgrad_ref, store_sem, rows_ref, cols_ref, count_ref,
     features, weight, bias, scale_ref, cotangent,
-    tiles, tiles_t, terms, out_row, out_col, in_row, in_col,
+    tiles, tiles_t, row_terms, col_terms, out_row, out_col, in_row, in_col,
     w_part, w_in, w_cross, w_all, load_sem, send_row_sem, send_col_sem, recv_row_sem, recv_col_sem,
     x_row0, x_row1, x_col0, x_col1,
 ):
@@ -98,7 +98,7 @@
         each(1, n_col, lambda k: col_copy(phase, k, xr.at[c], xr.at[c]).start())
         each(1, n_row, lambda k: row_copy(phase, k, xc.at[r], xc.at[r]).start())
 
-    def partial(at, index):
+    def partial(terms, at, index):
         total = None
         for t in range(slots):
             term = terms[t] * jnp.where(at[t] == index, weights[t], 0.0)
@@ -110,26 +110,31 @@
         stage = 2 + phase
         col_all(phase, xr).wait_recv()
         for t in range(slots):
-            terms[t] = dot(xr[row_at[t]], tiles[t])
+            col_terms[t] = dot(xr[row_at[t]], tiles[t])
+        row_all(phase, xc).wait_recv()
+        for t in range(slots):
+            row_terms[t] = dot(xc[col_at[t]], tiles_t[t])
+
+        def to_col(k):
+            out_row[phase, k] = partial(row_terms, row_at, col_peer(k))
+            col_copy(stage, k, out_row.at[phase, k], in_row.at[phase, c]).start()
 
         def to_row(k):
-            out_col[phase, k] = partial(col_at, row_peer(k))
+            out_col[phase, k] = partial(col_terms, col_at, row_peer(k))
             row_copy(stage, k, out_col.at[phase, k], in_col.at[phase, r]).start()
 
-        each(1, n_row, to_row)
-        in_col[phase, r] = partial(col_at, r)
+        def to_both(k):
+            to_col(k)
+            to_row(k)
+
+        common = min(n_row, n_col)
+        each(1, common, to_both)
+        each(common, n_col, to_col)
+        each(common, n_row, to_row)
+        in_row[phase, c] = partial(row_terms, row_at, c)
+        in_col[phase, r] = partial(col_terms, col_at, r)
         if between is not None:
             between()
-        row_all(phase, xc).wait_recv()
-        for t in range(slots):
-            terms[t] = dot(xc[col_at[t]], tiles_t[t])
-
-        def to_col(k):
-            out_row[phase, k] = partial(row_at, col_peer(k))
-            col_copy(stage, k, out_row.at[phase, k], in_row.at[phase, c]).start()
-
-        each(1, n_col, to_col)
-        in_row[phase, c] = partial(row_at, c)
 
     def collect(phase, own):
         total = own.astype(F32)
@@ -268,6 +273,7 @@
             pltpu.VMEM((BLOCK, width), BF16),
             pltpu.VMEM((slots, BLOCK, BLOCK), BF16),
             pltpu.VMEM((slots, BLOCK, BLOCK), BF16),
+            pltpu.VMEM((slots, width, BLOCK), F32),
             pltpu.VMEM((slots, width, BLOCK), F32),
             pltpu.VMEM((2, n_col, width, BLOCK), BF16),
             pltpu.VMEM((2, n_row, width, BLOCK), BF16),

time: 41.3 us -> 45.1 us (1.092)
  Pallas kernels: 39.8 us -> 43.7 us
    pallas_call x1, Pallas kernels: 38.2 us -> 42.1 us  [shards(): pl.pallas_call(functools.partial(layer_kernel, n_row, n_col, slots), out_...]
where the time goes in v5:
time: 45.1 us; the launch traced here: 44.9 us
  Pallas kernels  43.7 us (97%)
  between operations  1.29 us (3%)
    pallas_call x1, Pallas kernels, shards(): pl.pallas_call(functools.partial(layer_kernel, n_row, n_col, slots), out_...  42.1 us
    pallas_call x1, Pallas kernels, shards(): pl.pallas_call(functools.partial(finish_kernel, 4), out_shape=shapes, in_...  1.6 us

profile of v5, /device:TPU:0, one launch (start us, length us, event | category | flops | bytes accessed | tf_op | source)
XLA Modules:
  0.0 44.9 jit_solution(2522010977802527723)
XLA Ops:
  1.3 42.1 %shard_map.120 = (bf16[256,128]{1,0:T(8,128)(2,1)}, bf16[256,128]{1,0:T(8,128)(2,1)}, f32[128,128]{1,0:T(8,128)}, f32[1,128]{1,0:T(1,128)}) custom-call(s32[8]{0:T(128)} %bitcast.10, s32[8]{0:T(128)} %bitcast.11, s32[1]{0:T(128)} %bitcast.7.count_hbm, bf16[256,128]{1,0:T(8,128)(2,1)} %features_hbm.1, bf16[128,128]{1,0:T(8,128)(2,1)} %weight_hbm.1, ...), custom_call_target="tpu_custom_call" | custom-call | tf_op jit(solution)/shard_map/pallas_call | solution.py:258
  43.3 1.6 %shard_map.121 = (bf16[256,128]{1,0:T(8,128)(2,1)}, bf16[256,128]{1,0:T(8,128)(2,1)}, f32[128,128]{1,0:T(8,128)}, f32[1,128]{1,0:T(1,128)}) custom-call(bf16[256,128]{1,0:T(8,128)(2,1)} %get-tuple-element.12.refs_0_, bf16[256,128]{1,0:T(8,128)(2,1)} %get-tuple-element.13.refs_1_, f32[128,128]{1,0:T(8,128)} %get-tuple-element.14.refs_2_, ...), custom_call_target="tpu_custom_call" | custom-call | tf_op jit(solution)/shard_map/pallas_call | solution.py:304

commit v6 on v5

--- a/solution.py
+++ b/solution.py
@@ -25,8 +25,9 @@
     act_hbm, fgrad_hbm, wgrad_hbm, bgrad_hbm,
     act_ref, fgrad_ref, wgrad_ref, bgrad_ref, store_sem, rows_ref, cols_ref, count_ref,
     features, weight, bias, scale_ref, cotangent,
-    tiles, tiles_t, row_terms, col_terms, out_row, out_col, in_row, in_col,
+    tiles, tiles_t, row_terms, col_terms, out_row, out_col, in_row, in_col, pair,
     w_part, w_in, w_cross, w_all, load_sem, send_row_sem, send_col_sem, recv_row_sem, recv_col_sem,
+    send_sib_sem, recv_sib_sem,
     x_row0, x_row1, x_col0, x_col1,
 ):
     r = lax.axis_index("row")
@@ -49,6 +50,15 @@
     def col_peer(k):
         return lax.rem(c + k, n_col)
 
+    chips = n_row // 2
+    sibling = r + 1 - 2 * lax.rem(r, 2)
+
+    def mate(k):
+        return lax.rem(r + 2 * k, n_row)
+
+    def mate_sibling(k):
+        return lax.rem(sibling + 2 * k, n_row)
+
     def each(first, last, body):
         def step(k, carry):
             body(k)
@@ -70,6 +80,24 @@
         return pltpu.make_async_remote_copy(
             src_ref=src, dst_ref=dst, send_sem=send_col_sem.at[stage], recv_sem=recv_col_sem.at[stage],
             device_id=(r, col_peer(k)), device_id_type=MESH)
+
+    def mate_copy(stage, k, src, dst):
+        return pltpu.make_async_remote_copy(
+            src_ref=src, dst_ref=dst, send_sem=send_row_sem.at[stage], recv_sem=recv_row_sem.at[stage],
+            device_id=(mate(k), c), device_id_type=MESH)
+
+    def sibling_copy(stage, src, dst):
+        return pltpu.make_async_remote_copy(
+            src_ref=src, dst_ref=dst, send_sem=send_sib_sem.at[stage], recv_sem=recv_sib_sem.at[stage],
+            device_id=(sibling, c), device_id_type=MESH)
+
+    def mate_all(stage, buffer):
+        whole = buffer.at[pl.ds(0, chips - 1)]
+        return mate_copy(stage, 1, whole, whole)
+
+    def sibling_all(stage, buffer, count):
+        whole = buffer.at[pl.ds(0, count)]
+        return sibling_copy(stage, whole, whole)
 
     def row_all(stage, buffer):
         whole = buffer.at[pl.ds(0, n_row - 1)]
@@ -96,14 +124,20 @@
         if phase == 0:
             pl.semaphore_wait(barrier, n_row + n_col - 2)
         each(1, n_col, lambda k: col_copy(phase, k, xr.at[c], xr.at[c]).start())
-        each(1, n_row, lambda k: row_copy(phase, k, xc.at[r], xc.at[r]).start())
-
-    def partial(terms, at, index):
+        each(1, chips, lambda k: mate_copy(phase, k, xc.at[r], xc.at[r]).start())
+        sibling_copy(phase, xc.at[r], xc.at[r]).start()
+
+    def partial(terms, at, index, kind=BF16):
         total = None
         for t in range(slots):
             term = terms[t] * jnp.where(at[t] == index, weights[t], 0.0)
             total = term if total is None else total + term
-        return total.astype(BF16)
+        return total.astype(kind)
+
+    def forward(phase):
+        xc = x_col[phase]
+        mate_all(phase, xc).wait_recv()
+        each(1, chips, lambda k: sibling_copy(phase, xc.at[mate(k)], xc.at[mate(k)]).start())
 
     def spread(phase, between=None):
         xr, xc = x_row[phase], x_col[phase]
@@ -111,35 +145,41 @@
         col_all(phase, xr).wait_recv()
         for t in range(slots):
             col_terms[t] = dot(xr[row_at[t]], tiles[t])
-        row_all(phase, xc).wait_recv()
+
+        def to_pair(k):
+            out_col[phase, k] = partial(col_terms, col_at, mate_sibling(k))
+            sibling_copy(stage, out_col.at[phase, k], pair.at[phase, k]).start()
+
+        each(1, chips, to_pair)
+        out_col[phase, 0] = partial(col_terms, col_at, sibling)
+        sibling_copy(4 + phase, out_col.at[phase, 0], in_col.at[phase, chips]).start()
+        sibling_all(phase, xc, chips).wait_recv()
         for t in range(slots):
             row_terms[t] = dot(xc[col_at[t]], tiles_t[t])
 
         def to_col(k):
-            out_row[phase, k] = partial(row_terms, row_at, col_peer(k))
+            out_row[phase, k] = partial(row_terms, row_at, col_peer(k)).astype(BF16)
             col_copy(stage, k, out_row.at[phase, k], in_row.at[phase, c]).start()
 
-        def to_row(k):
-            out_col[phase, k] = partial(col_terms, col_at, row_peer(k))
-            row_copy(stage, k, out_col.at[phase, k], in_col.at[phase, r]).start()
-
-        def to_both(k):
-            to_col(k)
-            to_row(k)
-
-        common = min(n_row, n_col)
-        each(1, common, to_both)
-        each(common, n_col, to_col)
-        each(common, n_row, to_row)
+        each(1, n_col, to_col)
+        sibling_all(stage, pair.at[phase], chips - 1).wait_recv()
+
+        def to_mate(k):
+            mine = partial(col_terms, col_at, mate(k), F32) + pair[phase, k].astype(F32)
+            out_col[phase, chips + k] = mine.astype(BF16)
+            mate_copy(stage, k, out_col.at[phase, chips + k], in_col.at[phase, k]).start()
+
+        each(1, chips, to_mate)
+        in_col[phase, 0] = partial(col_terms, col_at, r)
         in_row[phase, c] = partial(row_terms, row_at, c)
-        in_col[phase, r] = partial(col_terms, col_at, r)
         if between is not None:
             between()
 
     def collect(phase, own):
         total = own.astype(F32)
-        row_all(2 + phase, in_col.at[phase]).wait_recv()
-        for k in range(n_row):
+        sibling_all(4 + phase, in_col.at[phase], 1).wait_recv()
+        mate_all(2 + phase, in_col.at[phase]).wait_recv()
+        for k in range(chips + 1):
             total = total + in_col[phase, k].astype(F32)
         col_all(2 + phase, in_row.at[phase]).wait_recv()
         for k in range(n_col):
@@ -169,6 +209,7 @@
         tiles_t[t] = tiles[t].T
 
     each(0, slots, transpose)
+    forward(0)
     spread(0)
     weight_t = weight[...].T
     bias_t = jnp.broadcast_to(bias[...], (BLOCK, width)).T
@@ -201,6 +242,7 @@
         w_cross[c] = summed
         each(1, n_col, lambda k: col_copy(4, k, w_cross.at[c], w_cross.at[c]).start())
 
+    forward(1)
     spread(1, sum_over_row)
     col_all(4, w_cross).wait_recv()
     summed = w_cross[0]
@@ -218,8 +260,12 @@
     for k in range(n_row):
         wgrad_ref[k * chunk:(k + 1) * chunk, :] = w_all[k, :chunk, :]
     store(2, wgrad_ref, wgrad_hbm)
-    for stage in range(6):
-        row_all(stage, x_col0 if stage < 4 else w_in).wait_send()
+    for stage in range(4):
+        mate_all(stage, x_col0).wait_send()
+    for stage in range(4, 6):
+        row_all(stage, w_in).wait_send()
+    for stage, count in enumerate((chips, chips, chips - 1, chips - 1, 1, 1)):
+        sibling_all(stage, x_col0, count).wait_send()
     for stage in range(5):
         col_all(stage, x_row0 if stage < 4 else w_cross).wait_send()
     for copy in stores:
@@ -278,7 +324,8 @@
             pltpu.VMEM((2, n_col, width, BLOCK), BF16),
             pltpu.VMEM((2, n_row, width, BLOCK), BF16),
             pltpu.VMEM((2, n_col, width, BLOCK), BF16),
-            pltpu.VMEM((2, n_row, width, BLOCK), BF16),
+            pltpu.VMEM((2, n_row // 2 + 1, width, BLOCK), BF16),
+            pltpu.VMEM((2, n_row // 2, width, BLOCK), BF16),
             pltpu.VMEM((n_row, chunk + 8, width), F32),
             pltpu.VMEM((n_row, chunk + 8, width), F32),
             pltpu.VMEM((n_col, chunk + 8, width), F32),
@@ -288,6 +335,8 @@
             pltpu.SemaphoreType.DMA((5,)),
             pltpu.SemaphoreType.DMA((6,)),
             pltpu.SemaphoreType.DMA((5,)),
+            pltpu.SemaphoreType.DMA((6,)),
+            pltpu.SemaphoreType.DMA((6,)),
             pltpu.VMEM((n_col, width, BLOCK), BF16),
             pltpu.VMEM((n_col, width, BLOCK), BF16),
             pltpu.VMEM((n_row, width, BLOCK), BF16),

time: 45.1 us -> 43.8 us (0.971)
  Pallas kernels: 43.7 us -> 42.3 us
    pallas_call x1, Pallas kernels: 42.1 us -> 40.7 us  [shards(): pl.pallas_call(functools.partial(layer_kernel, n_row, n_col, slots), out_...]
where the time goes in v6:
time: 43.8 us; the launch traced here: 43.6 us
  Pallas kernels  42.3 us (97%)
  between operations  1.29 us (3%)
    pallas_call x1, Pallas kernels, shards(): pl.pallas_call(functools.partial(layer_kernel, n_row, n_col, slots), out_...  40.7 us
    pallas_call x1, Pallas kernels, shards(): pl.pallas_call(functools.partial(finish_kernel, 4), out_shape=shapes, in_...  1.6 us

profile of v6, /device:TPU:0, one launch (start us, length us, event | category | flops | bytes accessed | tf_op | source)
XLA Modules:
  0.0 43.6 jit_solution(9452467384819884967)
XLA Ops:
  1.3 40.7 %shard_map.120 = (bf16[256,128]{1,0:T(8,128)(2,1)}, bf16[256,128]{1,0:T(8,128)(2,1)}, f32[128,128]{1,0:T(8,128)}, f32[1,128]{1,0:T(1,128)}) custom-call(s32[8]{0:T(128)} %bitcast.10, s32[8]{0:T(128)} %bitcast.11, s32[1]{0:T(128)} %bitcast.7.count_hbm, bf16[256,128]{1,0:T(8,128)(2,1)} %features_hbm.1, bf16[128,128]{1,0:T(8,128)(2,1)} %weight_hbm.1, ...), custom_call_target="tpu_custom_call" | custom-call | tf_op jit(solution)/shard_map/pallas_call | solution.py:304
  42.0 1.6 %shard_map.121 = (bf16[256,128]{1,0:T(8,128)(2,1)}, bf16[256,128]{1,0:T(8,128)(2,1)}, f32[128,128]{1,0:T(8,128)}, f32[1,128]{1,0:T(1,128)}) custom-call(bf16[256,128]{1,0:T(8,128)(2,1)} %get-tuple-element.12.refs_0_, bf16[256,128]{1,0:T(8,128)(2,1)} %get-tuple-element.13.refs_1_, f32[128,128]{1,0:T(8,128)} %get-tuple-element.14.refs_2_, ...), custom_call_target="tpu_custom_call" | custom-call | tf_op jit(solution)/shard_map/pallas_call | solution.py:353

commit v7 on v4

--- a/solution.py
+++ b/solution.py
@@ -27,6 +27,7 @@
     features, weight, bias, scale_ref, cotangent,
     tiles, tiles_t, terms, out_row, out_col, in_row, in_col,
     w_part, w_in, w_cross, w_all, load_sem, send_row_sem, send_col_sem, recv_row_sem, recv_col_sem,
+    send_sib_sem, recv_sib_sem,
     x_row0, x_row1, x_col0, x_col1,
 ):
     r = lax.axis_index("row")
@@ -49,6 +50,12 @@
     def col_peer(k):
         return lax.rem(c + k, n_col)
 
+    chips = n_row // 2
+    sibling = r + 1 - 2 * lax.rem(r, 2)
+
+    def mate(k):
+        return lax.rem(r + 2 * k, n_row)
+
     def each(first, last, body):
         def step(k, carry):
             body(k)
@@ -70,6 +77,24 @@
         return pltpu.make_async_remote_copy(
             src_ref=src, dst_ref=dst, send_sem=send_col_sem.at[stage], recv_sem=recv_col_sem.at[stage],
             device_id=(r, col_peer(k)), device_id_type=MESH)
+
+    def mate_copy(stage, k, src, dst):
+        return pltpu.make_async_remote_copy(
+            src_ref=src, dst_ref=dst, send_sem=send_row_sem.at[stage], recv_sem=recv_row_sem.at[stage],
+            device_id=(mate(k), c), device_id_type=MESH)
+
+    def sibling_copy(stage, src, dst):
+        return pltpu.make_async_remote_copy(
+            src_ref=src, dst_ref=dst, send_sem=send_sib_sem.at[stage], recv_sem=recv_sib_sem.at[stage],
+            device_id=(sibling, c), device_id_type=MESH)
+
+    def mate_all(stage, buffer):
+        whole = buffer.at[pl.ds(0, chips - 1)]
+        return mate_copy(stage, 1, whole, whole)
+
+    def sibling_all(stage, buffer, count):
+        whole = buffer.at[pl.ds(0, count)]
+        return sibling_copy(stage, whole, whole)
 
     def row_all(stage, buffer):
         whole = buffer.at[pl.ds(0, n_row - 1)]
@@ -96,7 +121,8 @@
         if phase == 0:
             pl.semaphore_wait(barrier, n_row + n_col - 2)
         each(1, n_col, lambda k: col_copy(phase, k, xr.at[c], xr.at[c]).start())
-        each(1, n_row, lambda k: row_copy(phase, k, xc.at[r], xc.at[r]).start())
+        each(1, chips, lambda k: mate_copy(phase, k, xc.at[r], xc.at[r]).start())
+        sibling_copy(phase, xc.at[r], xc.at[r]).start()
 
     def partial(at, index):
         total = None
@@ -105,6 +131,11 @@
             total = term if total is None else total + term
         return total.astype(BF16)
 
+    def forward(phase):
+        xc = x_col[phase]
+        mate_all(phase, xc).wait_recv()
+        each(1, chips, lambda k: sibling_copy(phase, xc.at[mate(k)], xc.at[mate(k)]).start())
+
     def spread(phase, between=None):
         xr, xc = x_row[phase], x_col[phase]
         stage = 2 + phase
@@ -120,7 +151,7 @@
         in_col[phase, r] = partial(col_at, r)
         if between is not None:
             between()
-        row_all(phase, xc).wait_recv()
+        sibling_all(phase, xc, chips).wait_recv()
         for t in range(slots):
             terms[t] = dot(xc[col_at[t]], tiles_t[t])
 
@@ -164,6 +195,7 @@
         tiles_t[t] = tiles[t].T
 
     each(0, slots, transpose)
+    forward(0)
     spread(0)
     weight_t = weight[...].T
     bias_t = jnp.broadcast_to(bias[...], (BLOCK, width)).T
@@ -196,6 +228,7 @@
         w_cross[c] = summed
         each(1, n_col, lambda k: col_copy(4, k, w_cross.at[c], w_cross.at[c]).start())
 
+    forward(1)
     spread(1, sum_over_row)
     col_all(4, w_cross).wait_recv()
     summed = w_cross[0]
@@ -213,7 +246,10 @@
     for k in range(n_row):
         wgrad_ref[k * chunk:(k + 1) * chunk, :] = w_all[k, :chunk, :]
     store(2, wgrad_ref, wgrad_hbm)
-    for stage in range(6):
+    for stage in range(2):
+        mate_all(stage, x_col0).wait_send()
+        sibling_all(stage, x_col0, chips).wait_send()
+    for stage in range(2, 6):
         row_all(stage, x_col0 if stage < 4 else w_in).wait_send()
     for stage in range(5):
         col_all(stage, x_row0 if stage < 4 else w_cross).wait_send()
@@ -282,6 +318,8 @@
             pltpu.SemaphoreType.DMA((5,)),
             pltpu.SemaphoreType.DMA((6,)),
             pltpu.SemaphoreType.DMA((5,)),
+            pltpu.SemaphoreType.DMA((2,)),
+            pltpu.SemaphoreType.DMA((2,)),
             pltpu.VMEM((n_col, width, BLOCK), BF16),
             pltpu.VMEM((n_col, width, BLOCK), BF16),
             pltpu.VMEM((n_row, width, BLOCK), BF16),

time: 41.3 us -> 40.6 us (0.983)
  Pallas kernels: 39.8 us -> 39.1 us
    pallas_call x1, Pallas kernels: 38.2 us -> 37.5 us  [shards(): pl.pallas_call(functools.partial(layer_kernel, n_row, n_col, slots), out_...]
where the time goes in v7:
time: 40.6 us; the launch traced here: 40.4 us
  Pallas kernels  39.1 us (96%)
  between operations  1.29 us (3%)
    pallas_call x1, Pallas kernels, shards(): pl.pallas_call(functools.partial(layer_kernel, n_row, n_col, slots), out_...  37.5 us
    pallas_call x1, Pallas kernels, shards(): pl.pallas_call(functools.partial(finish_kernel, 4), out_shape=shapes, in_...  1.6 us

profile of v7, /device:TPU:0, one launch (start us, length us, event | category | flops | bytes accessed | tf_op | source)
XLA Modules:
  0.0 40.4 jit_solution(11639254253486866805)
XLA Ops:
  1.3 37.5 %shard_map.120 = (bf16[256,128]{1,0:T(8,128)(2,1)}, bf16[256,128]{1,0:T(8,128)(2,1)}, f32[128,128]{1,0:T(8,128)}, f32[1,128]{1,0:T(1,128)}) custom-call(s32[8]{0:T(128)} %bitcast.10, s32[8]{0:T(128)} %bitcast.11, s32[1]{0:T(128)} %bitcast.7.count_hbm, bf16[256,128]{1,0:T(8,128)(2,1)} %features_hbm.1, bf16[128,128]{1,0:T(8,128)(2,1)} %weight_hbm.1, ...), custom_call_target="tpu_custom_call" | custom-call | tf_op jit(solution)/shard_map/pallas_call | solution.py:289
  38.8 1.6 %shard_map.121 = (bf16[256,128]{1,0:T(8,128)(2,1)}, bf16[256,128]{1,0:T(8,128)(2,1)}, f32[128,128]{1,0:T(8,128)}, f32[1,128]{1,0:T(1,128)}) custom-call(bf16[256,128]{1,0:T(8,128)(2,1)} %get-tuple-element.12.refs_0_, bf16[256,128]{1,0:T(8,128)(2,1)} %get-tuple-element.13.refs_1_, f32[128,128]{1,0:T(8,128)} %get-tuple-element.14.refs_2_, ...), custom_call_target="tpu_custom_call" | custom-call | tf_op jit(solution)/shard_map/pallas_call | solution.py:336
